TPU v7x, 256 devices: a whole 4x4x8 slice. The times are simulated.
256 devices in a mesh: mem: 8 (over y, x_lo), space: 32 (over z, x_hi, core).
Axes of the slice: x: 4 (x_hi: 2, x_lo: 2; x = x_hi * 2 + x_lo), y: 4, z: 8, core: 2. Of those that a mesh axis runs over, the one named last changes fastest.
Arguments:
- state: float32 [32, 5, 256, 16, 256], P('mem', None, 'space'), may hold values from -6 to 6
- diffusion: float32 [5], replicated, may hold values from 0.1 to 0.5
- radius: int32 [16], replicated, may hold values from 4 to 8, as said below
- obs_cells: int32 [32, 128], P('space'), may hold values from 0 to 2047
- obs_count: int32 [32], P('space'), may hold values from 1 to 128, as said below
- obs_value: float32 [32, 128], P('space'), may hold values from -4 to 12
- obs_error: float32 [32, 128], P('space'), may hold values from 0.5 to 2
Outputs:
- analysis: float32 [32, 5, 256, 16, 256], P('mem', None, 'space')
Inputs may be any that keep to these rules, and one draw needn't show every extreme that they name: Some level has radius exactly 8. Only the first obs_count[t] entries of a tile's lists are sites; some tile has exactly 128 sites.
All inputs are finite; a program needn't handle non-finite values.
Results may differ from a plain program's by a relative error of at most 0.0003.
Values sent between devices are 32-bit elements; how exact they have to be, the bound alone decides.
No kernel may reach another device: no remote copies, remote signals or barrier semaphores. Data moves between devices by JAX's collectives and lax.ppermute only.
A program may use at most 64 MiB of HBM per device.

v0:
```python
import jax
import jax.numpy as jnp
from jax import lax
from jax.sharding import PartitionSpec as P

time_step = 0.2
blend_share = 0.5


def with_halo(array, sides, width):
    for axis, dim in sides:
        size, length = (lax.axis_size(axis), array.shape[dim])
        up = [(i, (i + 1) % size) for i in range(size)]
        down = [(j, i) for i, j in up]
        last = lax.slice_in_dim(array, length - width, length, axis=dim)
        leading = lax.slice_in_dim(array, 0, width, axis=dim)
        before = lax.ppermute(last, axis, up)
        after = lax.ppermute(leading, axis, down)
        array = jnp.concatenate([before, array, after], axis=dim)
    return array


def advance(padded, diffuse_rate):
    interior = padded[..., 1:-1, :, :]
    east_side = padded[..., 2:, :, :]
    west_side = padded[..., :-2, :, :]
    north_side = jnp.roll(interior, -1, axis=-1)
    south_side = jnp.roll(interior, 1, axis=-1)
    wind_east = interior[..., 0:1, :, :, :]
    wind_north = interior[..., 1:2, :, :, :]
    transport = (
        wind_east * (east_side - west_side) * 0.5 + wind_north * (north_side - south_side) * 0.5
    )
    spread = east_side + west_side + north_side + south_side - 4.0 * interior
    return interior + time_step * (diffuse_rate * spread - transport)


def local(state, diffusion, radius, obs_cells, obs_count, obs_value, obs_error):
    members = state.shape[0]
    fields_count = state.shape[1]
    tile_width = state.shape[2]
    levels = state.shape[3]
    lat_cells = state.shape[4]
    diffuse_rate = diffusion.reshape(fields_count, 1, 1, 1)
    fields = state
    for sweep_index in range(2):
        padded = with_halo(fields, (("space", 2),), 1)
        fields = advance(padded, diffuse_rate)
    column = jnp.mean(fields[:, 2], axis=2).reshape(members, tile_width * lat_cells)
    site_cells = obs_cells[0]
    sites_max = site_cells.shape[0]
    observed = jnp.take(column, site_cells, axis=1)
    innovation = obs_value[0][None, :] - observed
    is_valid = (jnp.arange(sites_max, dtype=jnp.int32) < obs_count[0]).astype(jnp.float32)
    misfit = is_valid[None, :] * (innovation * innovation) / (obs_error[0] * obs_error[0])[None, :]
    site_east = (site_cells // lat_cells).astype(jnp.float32)
    site_north = (site_cells % lat_cells).astype(jnp.float32)
    packed = jnp.concatenate([misfit, site_east[None, :], site_north[None, :]], axis=0)[:, None, :]
    nearby = with_halo(packed, (("space", 1),), 1)
    offsets = jnp.arange(3, dtype=jnp.int32) - 1
    misfit3 = nearby[:members].reshape(members, 3 * sites_max)
    x_sites = (nearby[members].astype(jnp.int32) + offsets[:, None] * tile_width).reshape(-1)
    y_sites = nearby[members + 1].astype(jnp.int32).reshape(-1)
    cell_index = jnp.arange(tile_width * lat_cells, dtype=jnp.int32)
    cell_east = cell_index // lat_cells
    cell_north = cell_index % lat_cells
    delta_east = cell_east[:, None] - x_sites[None, :]
    delta_north = (
        cell_north[:, None] - y_sites[None, :] + lat_cells // 2
    ) % lat_cells - lat_cells // 2
    distance_sq = (delta_east * delta_east + delta_north * delta_north).astype(jnp.float32)
    radius_float = radius.astype(jnp.float32)
    inverse = 1.0 / (radius_float * radius_float)

    def level_weights(inverse_level):
        taper = jnp.maximum(0.0, 1.0 - distance_sq * inverse_level) ** 2
        return -0.5 * jnp.einsum("mo,co->mc", misfit3, taper, precision=lax.Precision.HIGHEST)

    log_weight = lax.map(level_weights, inverse)
    log_weight = log_weight.reshape(levels, members, tile_width, lat_cells).transpose(1, 2, 0, 3)
    best_log = lax.pmax(jnp.max(log_weight, axis=0), "mem")
    expo_weight = jnp.exp(log_weight - best_log[None])
    weighted = jnp.einsum("mxzy,mfxzy->fxzy", expo_weight, fields, precision=lax.Precision.HIGHEST)
    weight_total, weighted = lax.psum((jnp.sum(expo_weight, axis=0), weighted), "mem")
    local_mean = weighted / weight_total[None]
    return fields + blend_share * (local_mean[None] - fields)


def solution(mesh):
    return jax.shard_map(
        local,
        mesh=mesh,
        in_specs=(
            P("mem", None, "space", None, None),
            P(),
            P(),
            P("space", None),
            P("space"),
            P("space", None),
            P("space", None),
        ),
        out_specs=P("mem", None, "space", None, None),
        check_vma=False,
    )
```

profile of v0, /device:TPU:128, one launch (start us, length us, event | category | flops | bytes accessed | tf_op | source)
XLA Modules:
  0.0 353.0 jit_solution(8198006641233575647)
XLA Ops:
  7.7 2.1 collective-permute-start
  9.9 3.6 %fusion.63 = (f32[4,5,8,16,255]{4,3,2,1,0:T(8,128)S(1)}, f32[4,5,8,16,255]{4,3,2,1,0:T(8,128)S(1)}) fusion(f32[4,5,8,16,256]{4,3,2,1,0:T(8,128)} %param.9), kind=kLoop, calls=%fused_computation.104 | loop fusion | bytes 10444800 | tf_op jit(solution)/shard_map/jit(_roll_static)/slice | solution.py:27
  14.8 5.1 %collective-permute-done.1 = f32[4,5,1,16,256]{4,3,2,1,0:T(8,128)S(1)} collective-permute-done((f32[4,5,1,16,256]{4,3,2,1,0:T(8,128)S(1)}, f32[4,5,1,16,256]{4,3,2,1,0:T(8,128)S(1)}, u32[]{:S(2)}, u32[]{:S(2)}) %collective-permute-start.1) | collective-permute-done | bytes 327712 | tf_op jit(solution)/shard_map/ppermute | solution.py:17
  20.0 2.2 multiply_add_fusion.2
  24.3 3.8 %collective-permute-done.2 = f32[4,5,1,16,256]{4,3,2,1,0:T(8,128)S(1)} collective-permute-done((f32[4,5,1,16,256]{4,3,2,1,0:T(8,128)S(1)}, f32[4,5,1,16,256]{4,3,2,1,0:T(8,128)S(1)}, u32[]{:S(2)}, u32[]{:S(2)}) %collective-permute-start.2) | collective-permute-done | bytes 327712 | tf_op jit(solution)/shard_map/ppermute | solution.py:18
  28.2 5.6 %collective-permute-done.3 = f32[4,5,1,16,256]{4,3,2,1,0:T(8,128)S(1)} collective-permute-done((f32[4,5,1,16,256]{4,3,2,1,0:T(8,128)S(1)}, f32[4,5,1,16,256]{4,3,2,1,0:T(8,128)S(1)}, u32[]{:S(2)}, u32[]{:S(2)}) %collective-permute-start.3) | collective-permute-done | bytes 327712 | tf_op jit(solution)/shard_map/ppermute | solution.py:17
  33.8 2.2 multiply_add_fusion.1
  36.1 1.3 copy.27
  37.4 1.9 gather_fusion
  39.9 5.0 %collective-permute-start.5 = (f32[6,1,128]{2,0,1:T(8,128)S(1)}, f32[6,1,128]{2,0,1:T(8,128)S(1)}, u32[]{:S(2)}, u32[]{:S(2)}) collective-permute-start(f32[6,1,128]{2,0,1:T(8,128)S(1)} %maximum_bitcast_fusion), channel_id=1, source_target_pairs={{1,0},{2,1},{3,2},{4,3},{5,4},{6,5},{7,6},{8,7},{9,8},{10,9},{11,1... | collective-permute-start | bytes 9224 | tf_op jit(solution)/shard_map/ppermute | solution.py:18
  46.3 126.7 %while.11 = (s32[]{:T(128)}, f32[16,4,2048]{2,1,0:T(4,128)}, f32[16]{0:T(128)S(1)}, f32[4,384]{1,0:T(4,128)S(1)}, s32[384]{0:T(512)S(1)}, /*index=5*/s32[2048]{0...) while((s32[]{:T(128)}, f32[16,4,2048]{2,1,0:T(4,128)}, f32[16]{0:T(128)S(1)}, ...), condition=%wide.region_2.3_spmd.clone, body=%wide.region_1.2_spmd.clone.sunk | while | flops 55844864 | bytes 59497 | solution.py:79
  46.9 7.3 %fusion.71 = f32[16,4,2048]{2,1,0:T(4,128)} fusion(f32[16,4,2048]{2,1,0:T(4,128)} %get-tuple-element.174, s32[]{:T(128)} %get-tuple-element.173, f32[4,384]{1,0:T(4,128)S(1)} %get-tuple-element.185, s32[384]{0:T(512)S(1)} %get-tuple-element.188, s32[2048]{0:T(1024)S(1)} %get-tuple-element.189, s32[384]{0:T(512)S(1)} %get-tuple-element.186, ...), kind=kOutput, calls=%fused_computation.20.clone.1 | convolution fusion | flops 55844864 | bytes 59392 | tf_op jit(solution)/shard_map/while/body/eval_jaxpr/mo,co->mc/dot_general | solution.py:77
  54.8 7.3 %fusion.71 = f32[16,4,2048]{2,1,0:T(4,128)} fusion(f32[16,4,2048]{2,1,0:T(4,128)} %get-tuple-element.174, s32[]{:T(128)} %get-tuple-element.173, f32[4,384]{1,0:T(4,128)S(1)} %get-tuple-element.185, s32[384]{0:T(512)S(1)} %get-tuple-element.188, s32[2048]{0:T(1024)S(1)} %get-tuple-element.189, s32[384]{0:T(512)S(1)} %get-tuple-element.186, ...), kind=kOutput, calls=%fused_computation.20.clone.1 | convolution fusion | flops 55844864 | bytes 59392 | tf_op jit(solution)/shard_map/while/body/eval_jaxpr/mo,co->mc/dot_general | solution.py:77
  62.7 7.3 %fusion.71 = f32[16,4,2048]{2,1,0:T(4,128)} fusion(f32[16,4,2048]{2,1,0:T(4,128)} %get-tuple-element.174, s32[]{:T(128)} %get-tuple-element.173, f32[4,384]{1,0:T(4,128)S(1)} %get-tuple-element.185, s32[384]{0:T(512)S(1)} %get-tuple-element.188, s32[2048]{0:T(1024)S(1)} %get-tuple-element.189, s32[384]{0:T(512)S(1)} %get-tuple-element.186, ...), kind=kOutput, calls=%fused_computation.20.clone.1 | convolution fusion | flops 55844864 | bytes 59392 | tf_op jit(solution)/shard_map/while/body/eval_jaxpr/mo,co->mc/dot_general | solution.py:77
  70.7 7.3 %fusion.71 = f32[16,4,2048]{2,1,0:T(4,128)} fusion(f32[16,4,2048]{2,1,0:T(4,128)} %get-tuple-element.174, s32[]{:T(128)} %get-tuple-element.173, f32[4,384]{1,0:T(4,128)S(1)} %get-tuple-element.185, s32[384]{0:T(512)S(1)} %get-tuple-element.188, s32[2048]{0:T(1024)S(1)} %get-tuple-element.189, s32[384]{0:T(512)S(1)} %get-tuple-element.186, ...), kind=kOutput, calls=%fused_computation.20.clone.1 | convolution fusion | flops 55844864 | bytes 59392 | tf_op jit(solution)/shard_map/while/body/eval_jaxpr/mo,co->mc/dot_general | solution.py:77
  78.6 7.3 %fusion.71 = f32[16,4,2048]{2,1,0:T(4,128)} fusion(f32[16,4,2048]{2,1,0:T(4,128)} %get-tuple-element.174, s32[]{:T(128)} %get-tuple-element.173, f32[4,384]{1,0:T(4,128)S(1)} %get-tuple-element.185, s32[384]{0:T(512)S(1)} %get-tuple-element.188, s32[2048]{0:T(1024)S(1)} %get-tuple-element.189, s32[384]{0:T(512)S(1)} %get-tuple-element.186, ...), kind=kOutput, calls=%fused_computation.20.clone.1 | convolution fusion | flops 55844864 | bytes 59392 | tf_op jit(solution)/shard_map/while/body/eval_jaxpr/mo,co->mc/dot_general | solution.py:77
  86.5 7.3 %fusion.71 = f32[16,4,2048]{2,1,0:T(4,128)} fusion(f32[16,4,2048]{2,1,0:T(4,128)} %get-tuple-element.174, s32[]{:T(128)} %get-tuple-element.173, f32[4,384]{1,0:T(4,128)S(1)} %get-tuple-element.185, s32[384]{0:T(512)S(1)} %get-tuple-element.188, s32[2048]{0:T(1024)S(1)} %get-tuple-element.189, s32[384]{0:T(512)S(1)} %get-tuple-element.186, ...), kind=kOutput, calls=%fused_computation.20.clone.1 | convolution fusion | flops 55844864 | bytes 59392 | tf_op jit(solution)/shard_map/while/body/eval_jaxpr/mo,co->mc/dot_general | solution.py:77
  94.4 7.3 %fusion.71 = f32[16,4,2048]{2,1,0:T(4,128)} fusion(f32[16,4,2048]{2,1,0:T(4,128)} %get-tuple-element.174, s32[]{:T(128)} %get-tuple-element.173, f32[4,384]{1,0:T(4,128)S(1)} %get-tuple-element.185, s32[384]{0:T(512)S(1)} %get-tuple-element.188, s32[2048]{0:T(1024)S(1)} %get-tuple-element.189, s32[384]{0:T(512)S(1)} %get-tuple-element.186, ...), kind=kOutput, calls=%fused_computation.20.clone.1 | convolution fusion | flops 55844864 | bytes 59392 | tf_op jit(solution)/shard_map/while/body/eval_jaxpr/mo,co->mc/dot_general | solution.py:77
  102.3 7.3 %fusion.71 = f32[16,4,2048]{2,1,0:T(4,128)} fusion(f32[16,4,2048]{2,1,0:T(4,128)} %get-tuple-element.174, s32[]{:T(128)} %get-tuple-element.173, f32[4,384]{1,0:T(4,128)S(1)} %get-tuple-element.185, s32[384]{0:T(512)S(1)} %get-tuple-element.188, s32[2048]{0:T(1024)S(1)} %get-tuple-element.189, s32[384]{0:T(512)S(1)} %get-tuple-element.186, ...), kind=kOutput, calls=%fused_computation.20.clone.1 | convolution fusion | flops 55844864 | bytes 59392 | tf_op jit(solution)/shard_map/while/body/eval_jaxpr/mo,co->mc/dot_general | solution.py:77
  110.2 7.3 %fusion.71 = f32[16,4,2048]{2,1,0:T(4,128)} fusion(f32[16,4,2048]{2,1,0:T(4,128)} %get-tuple-element.174, s32[]{:T(128)} %get-tuple-element.173, f32[4,384]{1,0:T(4,128)S(1)} %get-tuple-element.185, s32[384]{0:T(512)S(1)} %get-tuple-element.188, s32[2048]{0:T(1024)S(1)} %get-tuple-element.189, s32[384]{0:T(512)S(1)} %get-tuple-element.186, ...), kind=kOutput, calls=%fused_computation.20.clone.1 | convolution fusion | flops 55844864 | bytes 59392 | tf_op jit(solution)/shard_map/while/body/eval_jaxpr/mo,co->mc/dot_general | solution.py:77
  118.2 7.3 %fusion.71 = f32[16,4,2048]{2,1,0:T(4,128)} fusion(f32[16,4,2048]{2,1,0:T(4,128)} %get-tuple-element.174, s32[]{:T(128)} %get-tuple-element.173, f32[4,384]{1,0:T(4,128)S(1)} %get-tuple-element.185, s32[384]{0:T(512)S(1)} %get-tuple-element.188, s32[2048]{0:T(1024)S(1)} %get-tuple-element.189, s32[384]{0:T(512)S(1)} %get-tuple-element.186, ...), kind=kOutput, calls=%fused_computation.20.clone.1 | convolution fusion | flops 55844864 | bytes 59392 | tf_op jit(solution)/shard_map/while/body/eval_jaxpr/mo,co->mc/dot_general | solution.py:77
  126.1 7.3 %fusion.71 = f32[16,4,2048]{2,1,0:T(4,128)} fusion(f32[16,4,2048]{2,1,0:T(4,128)} %get-tuple-element.174, s32[]{:T(128)} %get-tuple-element.173, f32[4,384]{1,0:T(4,128)S(1)} %get-tuple-element.185, s32[384]{0:T(512)S(1)} %get-tuple-element.188, s32[2048]{0:T(1024)S(1)} %get-tuple-element.189, s32[384]{0:T(512)S(1)} %get-tuple-element.186, ...), kind=kOutput, calls=%fused_computation.20.clone.1 | convolution fusion | flops 55844864 | bytes 59392 | tf_op jit(solution)/shard_map/while/body/eval_jaxpr/mo,co->mc/dot_general | solution.py:77
  134.0 7.3 %fusion.71 = f32[16,4,2048]{2,1,0:T(4,128)} fusion(f32[16,4,2048]{2,1,0:T(4,128)} %get-tuple-element.174, s32[]{:T(128)} %get-tuple-element.173, f32[4,384]{1,0:T(4,128)S(1)} %get-tuple-element.185, s32[384]{0:T(512)S(1)} %get-tuple-element.188, s32[2048]{0:T(1024)S(1)} %get-tuple-element.189, s32[384]{0:T(512)S(1)} %get-tuple-element.186, ...), kind=kOutput, calls=%fused_computation.20.clone.1 | convolution fusion | flops 55844864 | bytes 59392 | tf_op jit(solution)/shard_map/while/body/eval_jaxpr/mo,co->mc/dot_general | solution.py:77
  141.9 7.3 %fusion.71 = f32[16,4,2048]{2,1,0:T(4,128)} fusion(f32[16,4,2048]{2,1,0:T(4,128)} %get-tuple-element.174, s32[]{:T(128)} %get-tuple-element.173, f32[4,384]{1,0:T(4,128)S(1)} %get-tuple-element.185, s32[384]{0:T(512)S(1)} %get-tuple-element.188, s32[2048]{0:T(1024)S(1)} %get-tuple-element.189, s32[384]{0:T(512)S(1)} %get-tuple-element.186, ...), kind=kOutput, calls=%fused_computation.20.clone.1 | convolution fusion | flops 55844864 | bytes 59392 | tf_op jit(solution)/shard_map/while/body/eval_jaxpr/mo,co->mc/dot_general | solution.py:77
  149.8 7.3 %fusion.71 = f32[16,4,2048]{2,1,0:T(4,128)} fusion(f32[16,4,2048]{2,1,0:T(4,128)} %get-tuple-element.174, s32[]{:T(128)} %get-tuple-element.173, f32[4,384]{1,0:T(4,128)S(1)} %get-tuple-element.185, s32[384]{0:T(512)S(1)} %get-tuple-element.188, s32[2048]{0:T(1024)S(1)} %get-tuple-element.189, s32[384]{0:T(512)S(1)} %get-tuple-element.186, ...), kind=kOutput, calls=%fused_computation.20.clone.1 | convolution fusion | flops 55844864 | bytes 59392 | tf_op jit(solution)/shard_map/while/body/eval_jaxpr/mo,co->mc/dot_general | solution.py:77
  157.7 7.3 %fusion.71 = f32[16,4,2048]{2,1,0:T(4,128)} fusion(f32[16,4,2048]{2,1,0:T(4,128)} %get-tuple-element.174, s32[]{:T(128)} %get-tuple-element.173, f32[4,384]{1,0:T(4,128)S(1)} %get-tuple-element.185, s32[384]{0:T(512)S(1)} %get-tuple-element.188, s32[2048]{0:T(1024)S(1)} %get-tuple-element.189, s32[384]{0:T(512)S(1)} %get-tuple-element.186, ...), kind=kOutput, calls=%fused_computation.20.clone.1 | convolution fusion | flops 55844864 | bytes 59392 | tf_op jit(solution)/shard_map/while/body/eval_jaxpr/mo,co->mc/dot_general | solution.py:77
  165.7 7.3 %fusion.71 = f32[16,4,2048]{2,1,0:T(4,128)} fusion(f32[16,4,2048]{2,1,0:T(4,128)} %get-tuple-element.174, s32[]{:T(128)} %get-tuple-element.173, f32[4,384]{1,0:T(4,128)S(1)} %get-tuple-element.185, s32[384]{0:T(512)S(1)} %get-tuple-element.188, s32[2048]{0:T(1024)S(1)} %get-tuple-element.189, s32[384]{0:T(512)S(1)} %get-tuple-element.186, ...), kind=kOutput, calls=%fused_computation.20.clone.1 | convolution fusion | flops 55844864 | bytes 59392 | tf_op jit(solution)/shard_map/while/body/eval_jaxpr/mo,co->mc/dot_general | solution.py:77
  173.0 1.3 reshape.101
  175.0 81.3 %all-reduce.4.cloned.1.call-done = f32[8,16,256]{2,0,1:T(8,128)} async-done(((f32[8,16,256]{2,0,1:T(8,128)}), f32[8,16,256]{2,0,1:T(8,128)}) %all-reduce.4.cloned.1.call-update) | async-done | bytes 131088 | tf_op jit(solution)/shard_map/pmax | solution.py:81
  256.3 1.6 fusion.45
  259.6 82.5 %all-reduce.6.cloned.1.call-done = (f32[5,8,16,256]{3,2,1,0:T(8,128)}, f32[8,16,256]{2,0,1:T(8,128)}) async-done(((f32[5,8,16,256]{3,2,1,0:T(8,128)}, f32[8,16,256]{2,0,1:T(8,128)}), (f32[5,8,16,256]{3,2,1,0:T(8,128)}, f32[8,16,256]{2,0,1:T(8,128)})) %all-reduce.6.cloned.1.call-update) | async-done | bytes 786448 | tf_op jit(solution)/shard_map/psum | solution.py:84
  344.2 1.9 multiply_add_fusion
  (69 shorter events, 20.2 us)
Async XLA Ops:
  6.5 249.8 %all-reduce.4.cloned.1.call-start = ((), (), s32[]{:S(2)}) async-start(), calls=%async_computation | async-start | bytes 262144 | tf_op jit(solution)/shard_map/pmax | solution.py:81
  7.7 7.1 %collective-permute-start = (f32[4,5,1,16,256]{4,3,2,1,0:T(8,128)S(1)}, f32[4,5,1,16,256]{4,3,2,1,0:T(8,128)S(1)}, u32[]{:S(2)}, u32[]{:S(2)}) collective-permute-start(f32[4,5,1,16,256]{4,3,2,1,0:T(8,128)S(1)} %get-tuple-element.102), channel_id=1, source_target_pairs={{1,0},{2,1},{3,2},{4,3},{5,4},{6,5},{7,6},{8,7},{9,8},{10,9},{11,1... | collective-permute-start | bytes 983048 | tf_op jit(solution)/shard_map/ppermute | solution.py:18
  9.7 3.7 %copy-start = (f32[4,5,8,16,256]{4,3,2,1,0:T(8,128)S(1)}, f32[4,5,8,16,256]{4,3,2,1,0:T(8,128)}, u32[]{:S(2)}) copy-start(f32[4,5,8,16,256]{4,3,2,1,0:T(8,128)} %param.9) | copy-start | bytes 7864324
  9.8 3.8 %copy-start.3 = (s32[1,128]{1,0:T(1,128)S(1)}, s32[1,128]{1,0:T(1,128)}, u32[]{:S(2)}) copy-start(s32[1,128]{1,0:T(1,128)} %param.12) | copy-start | bytes 1540
  9.8 4.5 %copy-start.4 = (f32[1,128]{1,0:T(1,128)S(1)}, f32[1,128]{1,0:T(1,128)}, u32[]{:S(2)}) copy-start(f32[1,128]{1,0:T(1,128)} %param.15) | copy-start | bytes 1540
  9.8 4.5 %copy-start.5 = (s32[16]{0:T(128)S(1)}, s32[16]{0:T(128)}, u32[]{:S(2)}) copy-start(s32[16]{0:T(128)} %param.11) | copy-start | bytes 196
  9.8 10.2 %collective-permute-start.1 = (f32[4,5,1,16,256]{4,3,2,1,0:T(8,128)S(1)}, f32[4,5,1,16,256]{4,3,2,1,0:T(8,128)S(1)}, u32[]{:S(2)}, u32[]{:S(2)}) collective-permute-start(f32[4,5,1,16,256]{4,3,2,1,0:T(8,128)S(1)} %get-tuple-element.101), channel_id=1, source_target_pairs={{0,1},{1,2},{2,3},{3,4},{4,5},{5,6},{6,7},{7,8},{8,9},{9,10},{10,1... | collective-permute-start | bytes 983048 | tf_op jit(solution)/shard_map/ppermute | solution.py:17
  14.3 5.6 %copy-start.1 = (f32[5]{0:T(128)S(1)}, f32[5]{0:T(128)}, u32[]{:S(2)}) copy-start(f32[5]{0:T(128)} %param.10) | copy-start | bytes 64
  23.2 5.0 %collective-permute-start.2 = (f32[4,5,1,16,256]{4,3,2,1,0:T(8,128)S(1)}, f32[4,5,1,16,256]{4,3,2,1,0:T(8,128)S(1)}, u32[]{:S(2)}, u32[]{:S(2)}) collective-permute-start(f32[4,5,1,16,256]{4,3,2,1,0:T(8,128)S(1)} %get-tuple-element.94), channel_id=1, source_target_pairs={{1,0},{2,1},{3,2},{4,3},{5,4},{6,5},{7,6},{8,7},{9,8},{10,9},{11,1... | collective-permute-start | bytes 983048 | tf_op jit(solution)/shard_map/ppermute | solution.py:18
  23.5 10.2 %collective-permute-start.3 = (f32[4,5,1,16,256]{4,3,2,1,0:T(8,128)S(1)}, f32[4,5,1,16,256]{4,3,2,1,0:T(8,128)S(1)}, u32[]{:S(2)}, u32[]{:S(2)}) collective-permute-start(f32[4,5,1,16,256]{4,3,2,1,0:T(8,128)S(1)} %get-tuple-element.93), channel_id=1, source_target_pairs={{0,1},{1,2},{2,3},{3,4},{4,5},{5,6},{6,7},{7,8},{8,9},{9,10},{10,1... | collective-permute-start | bytes 983048 | tf_op jit(solution)/shard_map/ppermute | solution.py:17
  33.7 5.6 %copy-start.2 = (f32[1,128]{1,0:T(1,128)S(1)}, f32[1,128]{1,0:T(1,128)}, u32[]{:S(2)}) copy-start(f32[1,128]{1,0:T(1,128)} %param.14) | copy-start | bytes 1540
  39.4 6.7 %collective-permute-start.4 = (f32[6,1,128]{2,0,1:T(8,128)S(1)}, f32[6,1,128]{2,0,1:T(8,128)S(1)}, u32[]{:S(2)}, u32[]{:S(2)}) collective-permute-start(f32[6,1,128]{2,0,1:T(8,128)S(1)} %maximum_bitcast_fusion), channel_id=1, source_target_pairs={{0,1},{1,2},{2,3},{3,4},{4,5},{5,6},{6,7},{7,8},{8,9},{9,10},{10,1... | collective-permute-start | bytes 9224 | tf_op jit(solution)/shard_map/ppermute | solution.py:17
  39.9 6.3 %collective-permute-start.5 = (f32[6,1,128]{2,0,1:T(8,128)S(1)}, f32[6,1,128]{2,0,1:T(8,128)S(1)}, u32[]{:S(2)}, u32[]{:S(2)}) collective-permute-start(f32[6,1,128]{2,0,1:T(8,128)S(1)} %maximum_bitcast_fusion), channel_id=1, source_target_pairs={{1,0},{2,1},{3,2},{4,3},{5,4},{6,5},{7,6},{8,7},{9,8},{10,9},{11,1... | collective-permute-start | bytes 9224 | tf_op jit(solution)/shard_map/ppermute | solution.py:18
  175.0 167.1 %all-reduce.6.cloned.1.call-start = ((), (), s32[]{:S(2)}) async-start(), calls=%async_computation.1 | async-start | bytes 1572864 | tf_op jit(solution)/shard_map/psum | solution.py:84
Sparse Core Ops, SparseCore 0:
  175.1 81.1 all-reduce.3
  259.7 82.3 all-reduce.5
where the time goes:
time: 355 us; the launch traced here: 353 us
  waiting for transfers between devices  180 us (51%)
  matrix products  117 us (33%)
  local copies, waits for them, and re-layouts  22.4 us (6%)
  between operations  14.3 us (4%)
  other arithmetic  11.4 us (3%)
  starting transfers between devices  8.24 us (2%)
    dot_general x16, matrix products, level_weights(): jnp.einsum('mo,co->mc', misfit3, taper, precision=lax.Precision.HIGHEST)  117 us
    psum x1, waiting for transfers between devices, local(): lax.psum((jnp.sum(expo_weight, axis=0), weighted), 'mem')  82.5 us
    pmax x1, waiting for transfers between devices, local(): best_log = lax.pmax(jnp.max(log_weight, axis=0), 'mem')  81.3 us
    ppermute x3, waiting for transfers between devices, with_halo(): before = lax.ppermute(last, axis, up)  12 us
    dynamic_slice x16, local copies, waits for them, and re-layouts, local(): log_weight = lax.map(level_weights, inverse)  9.71 us
    ppermute x3, starting transfers between devices, with_halo(): after = lax.ppermute(leading, axis, down)  7.38 us
  transfers between devices with their start and end apart: 8, of which 6 were waited for; matrix products, arithmetic and copies ran while one was open for 1% of the time, Pallas kernels for 0%

commit v1 on v0

v1 whole, which is shorter than its diff:
```python
import jax
import jax.numpy as jnp
import numpy as np
from jax import lax
from jax.experimental import pallas as pl
from jax.experimental.pallas import tpu as pltpu
from jax.sharding import PartitionSpec as P

time_step = 0.2
blend_share = 0.5
radii = (4, 5, 6, 7, 8)
reach = 7
f32 = jnp.float32
edge_rows = (0, 1, 6, 7)
smem = pl.BlockSpec(memory_space=pltpu.SMEM)
vmem = pl.BlockSpec(memory_space=pltpu.VMEM)


def taper_of(distance_sq, radius):
    inverse = np.float32(1.0) / np.float32(radius * radius)
    share = max(np.float32(0.0), np.float32(1.0) - np.float32(distance_sq) * inverse)
    return float(np.float32(share * share))


def step_row(centre, west, east, u_part, v_part, rate):
    size = centre.shape[-1]
    north = pltpu.roll(centre, size - 1, 1)
    south = pltpu.roll(centre, 1, 1)
    spread = (east + west) + (north + south) - 4.0 * centre
    return centre + (rate * spread - (u_part * (east - west) + v_part * (north - south)))


def interior_kernel(state, diffusion, cells, count, value, error, once, inner, column, grids):
    sites = cells.shape[1]
    lat_cells = state.shape[4]
    half = 0.5 * time_step

    def member(m, carry):
        for f in range(5):
            rate = diffusion[f] * time_step
            for x in range(1, 7):
                once[m, f, x - 1] = step_row(
                    state[m, f, x],
                    state[m, f, x - 1],
                    state[m, f, x + 1],
                    half * state[m, 0, x],
                    half * state[m, 1, x],
                    rate,
                )
        for f in range(5):
            rate = diffusion[f] * time_step
            for x in range(2, 6):
                row = step_row(
                    once[m, f, x - 1],
                    once[m, f, x - 2],
                    once[m, f, x],
                    half * once[m, 0, x - 1],
                    half * once[m, 1, x - 1],
                    rate,
                )
                inner[m, f, x - 2] = row
                if f == 2:
                    column[m, pl.ds(x - 2, 1)] = jnp.mean(row, axis=0, keepdims=True)
        return carry

    lax.fori_loop(0, state.shape[0], member, 0)

    cell = cells[...]
    site_x = cell // lat_cells
    site_y = cell % lat_cells
    valid = lax.broadcasted_iota(jnp.int32, (1, sites), 1) < count[0]
    weight = jnp.where(valid, 1.0 / (error[...] * error[...]), 0.0)
    moments = jnp.concatenate([weight, weight * value[...], weight * value[...] * value[...]], axis=0)
    at_x = lax.broadcasted_iota(jnp.int32, (8, sites), 0) == site_x
    at_y = (lax.broadcasted_iota(jnp.int32, (lat_cells, sites), 0) == site_y).astype(f32)
    stacked = jnp.concatenate(
        [jnp.where(at_x, moments[k : k + 1], 0.0) for k in range(3)], axis=0
    )
    sums = lax.dot_general(
        stacked, at_y, (((1,), (1,)), ((), ())), precision=lax.Precision.HIGHEST, preferred_element_type=f32
    )
    total, first, second = sums[0:8], sums[8:16], sums[16:24]
    mean = jnp.where(total > 0.0, first / jnp.where(total > 0.0, total, 1.0), 0.0)
    grids[0] = total
    grids[1] = mean
    grids[2] = second - first * mean


def first_rows(m, f, h, state, west, east, winds, rate):
    far_w, near_w = west[m, h, 0], west[m, h, 1]
    near_e, far_e = east[m, h, 0], east[m, h, 1]
    return (
        step_row(near_w, far_w, state[m, f, 0], *winds[0], rate),
        step_row(state[m, f, 0], near_w, state[m, f, 1], *winds[1], rate),
        step_row(state[m, f, 7], state[m, f, 6], near_e, *winds[2], rate),
        step_row(near_e, state[m, f, 7], far_e, *winds[3], rate),
    )


def second_rows(m, f, rows, once, winds, rate):
    return (
        step_row(rows[1], rows[0], once[m, f, 0], *winds[0], rate),
        step_row(once[m, f, 0], rows[1], once[m, f, 1], *winds[1], rate),
        step_row(once[m, f, 5], once[m, f, 4], rows[2], *winds[2], rate),
        step_row(rows[2], once[m, f, 5], rows[3], *winds[3], rate),
    )


def raw_winds(m, state, west, east):
    half = 0.5 * time_step
    return tuple(
        (half * pair[0], half * pair[1])
        for pair in (
            (west[m, 0, 1], west[m, 1, 1]),
            (state[m, 0, 0], state[m, 1, 0]),
            (state[m, 0, 7], state[m, 1, 7]),
            (east[m, 0, 0], east[m, 1, 0]),
        )
    )


def edge_kernel(state, diffusion, west, east, once, column, grids, edge, winds_out, grid):
    half = 0.5 * time_step

    def member(m, carry):
        winds = raw_winds(m, state, west, east)
        rows = [
            first_rows(m, f, f, state, west, east, winds, diffusion[f] * time_step) for f in range(3)
        ]
        after = []
        for k, (u_row, v_row) in enumerate(
            (
                (rows[0][1], rows[1][1]),
                (once[m, 0, 0], once[m, 1, 0]),
                (once[m, 0, 5], once[m, 1, 5]),
                (rows[0][2], rows[1][2]),
            )
        ):
            pair = (half * u_row, half * v_row)
            winds_out[m, 0, k] = pair[0]
            winds_out[m, 1, k] = pair[1]
            after.append(pair)
        means = []
        for f in (2, 0, 1):
            done = second_rows(m, f, rows[f], once, after, diffusion[f] * time_step)
            for k in range(4):
                edge[m, f, k] = done[k]
                if f == 2:
                    means.append(jnp.mean(done[k], axis=0, keepdims=True))
        inside = column[m]
        full = jnp.concatenate([means[0], means[1], inside, means[2], means[3]], axis=0)
        off = full - grids[1]
        grid[m] = grids[0] * (off * off) + grids[2]
        return carry

    lax.fori_loop(0, state.shape[0], member, 0)


def edge_rest_kernel(state, diffusion, west_winds, east_winds, west, east, once, winds_in, edge):
    def member(m, carry):
        winds = raw_winds(m, state, west_winds, east_winds)
        after = [(winds_in[m, 0, k], winds_in[m, 1, k]) for k in range(4)]
        for f in (3, 4):
            rate = diffusion[f] * time_step
            rows = first_rows(m, f, f - 3, state, west, east, winds, rate)
            done = second_rows(m, f, rows, once, after, rate)
            for k in range(4):
                edge[m, f - 3, k] = done[k]
        return carry

    lax.fori_loop(0, state.shape[0], member, 0)


def by_level(rows, level_radius):
    result = jnp.broadcast_to(rows[0], level_radius.shape)
    for k in range(1, len(radii)):
        result = jnp.where(level_radius == radii[k], rows[k], result)
    return result


def weights_kernel(level_radius, own, before, after, inner, edge, rest, sends, near, shifted, expo):
    members, width, lat_cells = own.shape

    def convolve(m, carry):
        near[0:8] = before[m]
        near[8:16] = own[m]
        near[16:24] = after[m]
        grid = near[...]
        shifted[0] = grid
        for dy in range(1, reach + 1):
            shifted[dy] = pltpu.roll(grid, dy, 1) + pltpu.roll(grid, lat_cells - dy, 1)
        sums = [None] * len(radii)
        for dx in range(reach + 1):
            for dy in range(reach + 1):
                distance_sq = dx * dx + dy * dy
                if distance_sq >= radii[-1] ** 2:
                    continue
                if dx == 0:
                    pair = shifted[dy, 8:16]
                else:
                    pair = shifted[dy, 8 + dx : 16 + dx] + shifted[dy, 8 - dx : 16 - dx]
                for k, radius in enumerate(radii):
                    if distance_sq < radius * radius:
                        term = pair * (-0.5 * taper_of(distance_sq, radius))
                        sums[k] = term if sums[k] is None else sums[k] + term
        for k in range(len(radii)):
            expo[m, k] = sums[k]
        return carry

    lax.fori_loop(0, members, convolve, 0)
    for k in range(len(radii)):
        logs = [expo[m, k] for m in range(members)]
        best = logs[0]
        for m in range(1, members):
            best = jnp.maximum(best, logs[m])
        total = None
        for m in range(members):
            value = jnp.exp(logs[m] - best)
            expo[m, k] = value
            total = value if total is None else total + value
        for x in range(width):
            sends[x, 80 + k : 81 + k] = best[x : x + 1]
            sends[x, 85 + k : 86 + k] = total[x : x + 1]
    for x in range(width):
        sends[x, 90:96] = jnp.zeros((6, lat_cells), f32)
        sums = [None] * 5
        for m in range(members):
            weight = by_level([expo[m, k, x : x + 1] for k in range(len(radii))], level_radius[...])
            for f in range(5):
                if x in edge_rows:
                    k = edge_rows.index(x)
                    row = edge[m, f, k] if f < 3 else rest[m, f - 3, k]
                else:
                    row = inner[m, f, x - 2]
                term = weight * row
                sums[f] = term if sums[f] is None else sums[f] + term
        for f in range(5):
            sends[x, 16 * f : 16 * f + 16] = sums[f]


def combine_kernel(level_radius, parts, result):
    sources = parts.shape[0]
    logs = [parts[d, 80:85] for d in range(sources)]
    best = logs[0]
    for d in range(1, sources):
        best = jnp.maximum(best, logs[d])
    scales = [jnp.exp(logs[d] - best) for d in range(sources)]
    total = None
    for d in range(sources):
        term = scales[d] * parts[d, 85:90]
        total = term if total is None else total + term
    over = 1.0 / total
    sums = [None] * 5
    for d in range(sources):
        share = scales[d] * over
        weight = by_level([share[k : k + 1] for k in range(len(radii))], level_radius[...])
        for f in range(5):
            term = weight * parts[d, 16 * f : 16 * f + 16]
            sums[f] = term if sums[f] is None else sums[f] + term
    for f in range(5):
        for d in range(sources):
            result[d, 16 * f : 16 * f + 16] = sums[f]


def blend_kernel(mean, inner, edge, rest, out):
    for f in range(5):
        for x in range(8):
            if x in edge_rows:
                k = edge_rows.index(x)
                row = edge[0, f, k] if f < 3 else rest[0, f - 3, k]
            else:
                row = inner[0, f, x - 2]
            out[0, f, x] = row + blend_share * (mean[x, 16 * f : 16 * f + 16] - row)


def local(state, diffusion, radius, obs_cells, obs_count, obs_value, obs_error):
    members, fields, width, levels, lat_cells = state.shape
    size = lax.axis_size("space")
    up = [(i, (i + 1) % size) for i in range(size)]
    down = [(j, i) for i, j in up]

    def shape(*dims):
        return jax.ShapeDtypeStruct(dims, f32)

    west_a = lax.ppermute(state[:, :3, 6:8], "space", up)
    east_a = lax.ppermute(state[:, :3, 0:2], "space", down)
    west_b = lax.ppermute(state[:, 3:, 6:8], "space", up)
    east_b = lax.ppermute(state[:, 3:, 0:2], "space", down)
    level_radius = jnp.broadcast_to(radius[:, None], (levels, lat_cells))

    once, inner, column, grids = pl.pallas_call(
        interior_kernel,
        out_shape=(
            shape(members, fields, 6, levels, lat_cells),
            shape(members, fields, 4, levels, lat_cells),
            shape(members, 4, lat_cells),
            shape(3, width, lat_cells),
        ),
        in_specs=[vmem, smem, vmem, smem, vmem, vmem],
        name="interior",
    )(state, diffusion, obs_cells, obs_count, obs_value, obs_error)
    edge, winds, grid = pl.pallas_call(
        edge_kernel,
        out_shape=(
            shape(members, 3, 4, levels, lat_cells),
            shape(members, 2, 4, levels, lat_cells),
            shape(members, width, lat_cells),
        ),
        in_specs=[vmem, smem] + [vmem] * 5,
        name="edges",
    )(state, diffusion, west_a, east_a, once, column, grids)
    before = lax.ppermute(grid, "space", up)
    after = lax.ppermute(grid, "space", down)
    rest = pl.pallas_call(
        edge_rest_kernel,
        out_shape=shape(members, 2, 4, levels, lat_cells),
        in_specs=[vmem, smem] + [vmem] * 6,
        name="edges_rest",
    )(state, diffusion, west_a, east_a, west_b, east_b, once, winds)
    sends = pl.pallas_call(
        weights_kernel,
        out_shape=shape(width, 96, lat_cells),
        in_specs=[vmem] * 7,
        scratch_shapes=[
            pltpu.VMEM((24, lat_cells), f32),
            pltpu.VMEM((8, 24, lat_cells), f32),
            pltpu.VMEM((members, len(radii), width, lat_cells), f32),
        ],
        name="weights",
    )(level_radius, grid, before, after, inner, edge, rest)
    parts = lax.all_to_all(sends, "mem", 0, 0, tiled=True)
    share = pl.pallas_call(
        combine_kernel, out_shape=shape(width, 80, lat_cells), in_specs=[vmem] * 2, name="combine"
    )(level_radius, parts)
    mean = lax.all_to_all(share, "mem", 0, 0, tiled=True)

    def per_member(*dims):
        return pl.BlockSpec((1,) + dims, lambda m: (m, 0, 0, 0, 0))

    return pl.pallas_call(
        blend_kernel,
        grid=(members,),
        out_shape=shape(*state.shape),
        in_specs=[
            pl.BlockSpec((width, 80, lat_cells), lambda m: (0, 0, 0)),
            per_member(fields, 4, levels, lat_cells),
            per_member(3, 4, levels, lat_cells),
            per_member(2, 4, levels, lat_cells),
        ],
        out_specs=per_member(fields, width, levels, lat_cells),
        name="blend",
    )(mean, inner, edge, rest)


def solution(mesh):
    return jax.shard_map(
        local,
        mesh=mesh,
        in_specs=(
            P("mem", None, "space", None, None),
            P(),
            P(),
            P("space", None),
            P("space"),
            P("space", None),
            P("space", None),
        ),
        out_specs=P("mem", None, "space", None, None),
        check_vma=False,
    )
```

time: 355 us -> 78.3 us (0.22)
  waiting for transfers between devices: 180 us -> 0.02 us
  matrix products: 117 us -> 0 us
  blocking collectives: 0 us -> 29.3 us
  Pallas kernels: 0 us -> 26.2 us
  local copies, waits for them, and re-layouts: 22.4 us -> 4.58 us
  between operations: 14.3 us -> 0.75 us
  other arithmetic: 11.4 us -> 0 us
  starting transfers between devices: 8.24 us -> 16.2 us
    dot_general x16 -> x0, matrix products: 117 us -> none  [level_weights(): jnp.einsum('mo,co->mc', misfit3, taper, precision=lax.Precision.HIGHEST)]
    psum x1 -> x0, waiting for transfers between devices: 82.5 us -> none  [local(): lax.psum((jnp.sum(expo_weight, axis=0), weighted), 'mem')]
    pmax x1 -> x0, waiting for transfers between devices: 81.3 us -> none  [local(): best_log = lax.pmax(jnp.max(log_weight, axis=0), 'mem')]
    all_to_all x0 -> x2, blocking collectives: none -> 29.3 us  [the longest x1 15.6 us: local(): parts = lax.all_to_all(sends, 'mem', 0, 0, tiled=True)]
    pallas_call x0 -> x6, Pallas kernels: none -> 26.2 us  [the longest x1 5.71 us: local(): pl.pallas_call(interior_kernel, out_shape=(shape(members, fields, 6, leve...]
    ppermute x6, waiting for transfers between devices: 15.9 us -> 0.02 us  [the longest x1 0.01 us: local(): west_a = lax.ppermute(state[:, :3, 6:8], 'space', up)]
    dynamic_slice x16 -> x0, local copies, waits for them, and re-layouts: 9.71 us -> none  [local(): log_weight = lax.map(level_weights, inverse)]
    ppermute x6, starting transfers between devices: 8.19 us -> 16.2 us  [the longest x1 5.36 us: local(): after = lax.ppermute(grid, 'space', down)]
  transfers between devices with their start and end apart: 8 -> 6, of which waited for: 6 -> 0; matrix products, arithmetic and copies ran while one was open for 1% -> 1% of each run, Pallas kernels for 0% -> 20%
where the time goes in v1:
time: 78.3 us; the launch traced here: 77 us
  blocking collectives  29.3 us (37%)
  Pallas kernels  26.2 us (33%)
  starting transfers between devices  16.2 us (21%)
  local copies, waits for them, and re-layouts  4.58 us (6%)
    all_to_all x1, blocking collectives, local(): parts = lax.all_to_all(sends, 'mem', 0, 0, tiled=True)  15.6 us
    all_to_all x1, blocking collectives, local(): mean = lax.all_to_all(share, 'mem', 0, 0, tiled=True)  13.7 us
    pallas_call x1, Pallas kernels, local(): pl.pallas_call(interior_kernel, out_shape=(shape(members, fields, 6, leve...  5.71 us
    ppermute x1, starting transfers between devices, local(): after = lax.ppermute(grid, 'space', down)  5.36 us
    ppermute x1, starting transfers between devices, local(): east_a = lax.ppermute(state[:, :3, 0:2], 'space', down)  5.35 us
    ppermute x1, starting transfers between devices, local(): east_b = lax.ppermute(state[:, 3:, 0:2], 'space', down)  5.35 us
    pallas_call x1, Pallas kernels, local(): pl.pallas_call(edge_kernel, out_shape=(shape(members, 3, 4, levels, lat_c...  4.88 us
    pallas_call x1, Pallas kernels, local(): pl.pallas_call(weights_kernel, out_shape=shape(width, 96, lat_cells), in_...  4.63 us
  transfers between devices with their start and end apart: 6, of which 0 were waited for; matrix products, arithmetic and copies ran while one was open for 1% of the time, Pallas kernels for 20%

profile of v1, /device:TPU:128, one launch (start us, length us, event | category | flops | bytes accessed | tf_op | source)
XLA Modules:
  0.0 77.0 jit_solution(11527978644513829268)
XLA Ops:
  0.0 1.2 %fusion.1 = (f32[4,3,2,16,256]{4,3,2,1,0:T(8,128)S(1)}, f32[4,3,2,16,256]{4,3,2,1,0:T(8,128)S(1)}) fusion(f32[4,5,8,16,256]{4,3,2,1,0:T(8,128)} %state.5), kind=kLoop, calls=%fused_computation.1 | loop fusion | bytes 1572864 | tf_op jit(solution)/shard_map/slice | solution.py:286
  1.2 0.1 collective-permute-start
  1.3 5.3 %collective-permute-start.1 = (f32[4,3,2,16,256]{4,3,2,1,0:T(8,128)S(1)}, f32[4,3,2,16,256]{4,3,2,1,0:T(8,128)S(1)}, u32[]{:S(2)}, u32[]{:S(2)}) collective-permute-start(f32[4,3,2,16,256]{4,3,2,1,0:T(8,128)S(1)} %get-tuple-element.21), channel_id=1, source_target_pairs={{1,0},{2,1},{3,2},{4,3},{5,4},{6,5},{7,6},{8,7},{9,8},{10,9},{11,1... | collective-permute-start | bytes 1179656 | tf_op jit(solution)/shard_map/ppermute | solution.py:286
  6.6 1.1 %fusion = (f32[4,2,2,16,256]{4,3,2,1,0:T(8,128)S(1)}, f32[4,2,2,16,256]{4,3,2,1,0:T(8,128)S(1)}) fusion(f32[4,5,8,16,256]{4,3,2,1,0:T(8,128)} %state.5), kind=kLoop, calls=%fused_computation | loop fusion | bytes 1048576 | tf_op jit(solution)/shard_map/slice | solution.py:288
  7.7 0.1 collective-permute-start.4
  7.8 5.3 %collective-permute-start.5 = (f32[4,2,2,16,256]{4,3,2,1,0:T(8,128)S(1)}, f32[4,2,2,16,256]{4,3,2,1,0:T(8,128)S(1)}, u32[]{:S(2)}, u32[]{:S(2)}) collective-permute-start(f32[4,2,2,16,256]{4,3,2,1,0:T(8,128)S(1)} %get-tuple-element.19), channel_id=1, source_target_pairs={{1,0},{2,1},{3,2},{4,3},{5,4},{6,5},{7,6},{8,7},{9,8},{10,9},{11,1... | collective-permute-start | bytes 786440 | tf_op jit(solution)/shard_map/ppermute | solution.py:288
  13.8 5.7 %interior.1 = (f32[4,5,6,16,256]{4,3,2,1,0:T(8,128)}, f32[4,5,4,16,256]{4,3,2,1,0:T(8,128)}, f32[4,4,256]{2,1,0:T(4,128)}, f32[3,8,256]{2,1,0:T(8,128)}) custom-call(f32[4,5,8,16,256]{4,3,2,1,0:T(8,128)} %state.5, f32[5]{0:T(128)} %diffusion.5, s32[1,128]{1,0:T(1,128)} %cells.1, s32[1]{0:T(128)S(6)} %copy.8.count, f32[1,128]{1,0:T(1,128)} %value.1, ...), custom_call_target="tpu_custom_call" | custom-call | tf_op jit(solution)/shard_map/interior/pallas_call | solution.py:291
  19.5 0.0 collective-permute-done.west.west_winds
  19.5 0.0 collective-permute-done.1.east.east_winds
  19.5 0.0 copy-start.1
  19.5 0.7 copy-done
  20.2 0.2 copy-done.1
  20.4 4.9 %edges.1 = (f32[4,3,4,16,256]{4,3,2,1,0:T(8,128)}, f32[4,2,4,16,256]{4,3,2,1,0:T(8,128)}, f32[4,8,256]{2,1,0:T(8,128)}) custom-call(f32[4,5,8,16,256]{4,3,2,1,0:T(8,128)} %state.5, f32[5]{0:T(128)} %diffusion.5, f32[4,3,2,16,256]{4,3,2,1,0:T(8,128)} %copy-done, f32[4,3,2,16,256]{4,3,2,1,0:T(8,128)} %copy-done.1, ...), custom_call_target="tpu_custom_call" | custom-call | tf_op jit(solution)/shard_map/edges/pallas_call | solution.py:302
  25.3 0.0 collective-permute-start.2
  25.3 5.4 %collective-permute-start.3 = (f32[4,8,256]{2,1,0:T(8,128)}, f32[4,8,256]{2,1,0:T(8,128)S(1)}, u32[]{:S(2)}, u32[]{:S(2)}) collective-permute-start(f32[4,8,256]{2,1,0:T(8,128)} %get-tuple-element.15.own), channel_id=1, source_target_pairs={{1,0},{2,1},{3,2},{4,3},{5,4},{6,5},{7,6},{8,7},{9,8},{10,9},{11,1... | collective-permute-start | bytes 98312 | tf_op jit(solution)/shard_map/ppermute | solution.py:313
  30.6 0.0 collective-permute-done.4.west
  30.6 0.0 collective-permute-done.5.east
  30.6 0.0 copy-start.3
  30.7 0.7 copy-done.2
  31.4 0.1 copy-done.3
  31.4 4.6 %edges_rest.1.rest = f32[4,2,4,16,256]{4,3,2,1,0:T(8,128)} custom-call(f32[4,5,8,16,256]{4,3,2,1,0:T(8,128)} %state.5, f32[5]{0:T(128)} %diffusion.5, f32[4,3,2,16,256]{4,3,2,1,0:T(8,128)} %copy-done, f32[4,3,2,16,256]{4,3,2,1,0:T(8,128)} %copy-done.1, f32[4,2,2,16,256]{4,3,2,1,0:T(8,128)} %copy-done.2, f32[4,2,2,16,256]{4,3,2,1,0:T(8,128)} %copy-done.3, ...), custom_call_target="tpu_custom_call" | custom-call | tf_op jit(solution)/shard_map/edges_rest/pallas_call | solution.py:314
  36.0 0.0 collective-permute-done.2.before
  36.0 0.0 collective-permute-done.3.after
  36.0 0.0 copy-start.5
  36.0 0.0 copy-done.6
  36.0 0.7 broadcast_in_dim.2.level_radius
  36.7 0.0 copy-done.4
  36.7 4.6 %weights.1 = f32[8,96,256]{2,1,0:T(8,128)} custom-call(s32[16,256]{1,0:T(8,128)} %broadcast_in_dim.2.level_radius, f32[4,8,256]{2,1,0:T(8,128)} %get-tuple-element.15.own, f32[4,8,256]{2,1,0:T(8,128)} %copy-done.4, f32[4,8,256]{2,1,0:T(8,128)} %copy-done.5, f32[4,5,4,16,256]{4,3,2,1,0:T(8,128)} %get-tuple-element.16.inner, ...), custom_call_target="tpu_custom_call" | custom-call | tf_op jit(solution)/shard_map/weights/pallas_call | solution.py:320
  41.3 15.6 %all_to_all.10.parts = f32[8,96,256]{2,1,0:T(8,128)} all-to-all(f32[8,96,256]{2,1,0:T(8,128)} %weights.1), channel_id=1, replica_groups=mesh['mem'=8,'space'=32] {'mem'}, dimensions={0} | all-to-all | bytes 1572864 | tf_op jit(solution)/shard_map/all_to_all | solution.py:331
  56.9 2.1 %combine.1 = f32[8,80,256]{2,1,0:T(8,128)} custom-call(s32[16,256]{1,0:T(8,128)} %broadcast_in_dim.2.level_radius, f32[8,96,256]{2,1,0:T(8,128)} %all_to_all.10.parts), custom_call_target="tpu_custom_call" | custom-call | tf_op jit(solution)/shard_map/combine/pallas_call | solution.py:332
  59.0 13.7 %all_to_all.11.mean = f32[8,80,256]{2,1,0:T(8,128)} all-to-all(f32[8,80,256]{2,1,0:T(8,128)} %combine.1), channel_id=1, replica_groups=mesh['mem'=8,'space'=32] {'mem'}, dimensions={0} | all-to-all | bytes 1310720 | tf_op jit(solution)/shard_map/all_to_all | solution.py:335
  72.7 4.3 %blend.1 = f32[4,5,8,16,256]{4,3,2,1,0:T(8,128)} custom-call(f32[8,80,256]{2,1,0:T(8,128)} %all_to_all.11.mean, f32[4,5,4,16,256]{4,3,2,1,0:T(8,128)} %get-tuple-element.16.inner, f32[4,3,4,16,256]{4,3,2,1,0:T(8,128)} %get-tuple-element.17.edge, f32[4,2,4,16,256]{4,3,2,1,0:T(8,128)} %edges_rest.1.rest), custom_call_target="tpu_custom_call" | custom-call | tf_op jit(solution)/shard_map/blend/pallas_call | solution.py:340
  (5 shorter events, 0.0 us)
Async XLA Ops:
  1.2 18.3 %collective-permute-start = (f32[4,3,2,16,256]{4,3,2,1,0:T(8,128)S(1)}, f32[4,3,2,16,256]{4,3,2,1,0:T(8,128)S(1)}, u32[]{:S(2)}, u32[]{:S(2)}) collective-permute-start(f32[4,3,2,16,256]{4,3,2,1,0:T(8,128)S(1)} %get-tuple-element.22), channel_id=1, source_target_pairs={{0,1},{1,2},{2,3},{3,4},{4,5},{5,6},{6,7},{7,8},{8,9},{9,10},{10,1... | collective-permute-start | bytes 1179656 | tf_op jit(solution)/shard_map/ppermute | solution.py:285
  1.3 18.2 %collective-permute-start.1 = (f32[4,3,2,16,256]{4,3,2,1,0:T(8,128)S(1)}, f32[4,3,2,16,256]{4,3,2,1,0:T(8,128)S(1)}, u32[]{:S(2)}, u32[]{:S(2)}) collective-permute-start(f32[4,3,2,16,256]{4,3,2,1,0:T(8,128)S(1)} %get-tuple-element.21), channel_id=1, source_target_pairs={{1,0},{2,1},{3,2},{4,3},{5,4},{6,5},{7,6},{8,7},{9,8},{10,9},{11,1... | collective-permute-start | bytes 1179656 | tf_op jit(solution)/shard_map/ppermute | solution.py:286
  7.7 22.9 %collective-permute-start.4 = (f32[4,2,2,16,256]{4,3,2,1,0:T(8,128)S(1)}, f32[4,2,2,16,256]{4,3,2,1,0:T(8,128)S(1)}, u32[]{:S(2)}, u32[]{:S(2)}) collective-permute-start(f32[4,2,2,16,256]{4,3,2,1,0:T(8,128)S(1)} %get-tuple-element.20), channel_id=1, source_target_pairs={{0,1},{1,2},{2,3},{3,4},{4,5},{5,6},{6,7},{7,8},{8,9},{9,10},{10,1... | collective-permute-start | bytes 786440 | tf_op jit(solution)/shard_map/ppermute | solution.py:287
  7.8 22.9 %collective-permute-start.5 = (f32[4,2,2,16,256]{4,3,2,1,0:T(8,128)S(1)}, f32[4,2,2,16,256]{4,3,2,1,0:T(8,128)S(1)}, u32[]{:S(2)}, u32[]{:S(2)}) collective-permute-start(f32[4,2,2,16,256]{4,3,2,1,0:T(8,128)S(1)} %get-tuple-element.19), channel_id=1, source_target_pairs={{1,0},{2,1},{3,2},{4,3},{5,4},{6,5},{7,6},{8,7},{9,8},{10,9},{11,1... | collective-permute-start | bytes 786440 | tf_op jit(solution)/shard_map/ppermute | solution.py:288
  19.5 0.7 copy-start
  19.5 0.9 %copy-start.1 = (f32[4,3,2,16,256]{4,3,2,1,0:T(8,128)}, f32[4,3,2,16,256]{4,3,2,1,0:T(8,128)S(1)}, u32[]{:S(2)}) copy-start(f32[4,3,2,16,256]{4,3,2,1,0:T(8,128)S(1)} %collective-permute-done.1.east.east_winds) | copy-start | bytes 1179652
  25.3 10.7 %collective-permute-start.2 = (f32[4,8,256]{2,1,0:T(8,128)}, f32[4,8,256]{2,1,0:T(8,128)S(1)}, u32[]{:S(2)}, u32[]{:S(2)}) collective-permute-start(f32[4,8,256]{2,1,0:T(8,128)} %get-tuple-element.15.own), channel_id=1, source_target_pairs={{0,1},{1,2},{2,3},{3,4},{4,5},{5,6},{6,7},{7,8},{8,9},{9,10},{10,1... | collective-permute-start | bytes 98312 | tf_op jit(solution)/shard_map/ppermute | solution.py:312
  25.3 10.7 %collective-permute-start.3 = (f32[4,8,256]{2,1,0:T(8,128)}, f32[4,8,256]{2,1,0:T(8,128)S(1)}, u32[]{:S(2)}, u32[]{:S(2)}) collective-permute-start(f32[4,8,256]{2,1,0:T(8,128)} %get-tuple-element.15.own), channel_id=1, source_target_pairs={{1,0},{2,1},{3,2},{4,3},{5,4},{6,5},{7,6},{8,7},{9,8},{10,9},{11,1... | collective-permute-start | bytes 98312 | tf_op jit(solution)/shard_map/ppermute | solution.py:313
  30.6 0.7 copy-start.2
  30.6 0.8 %copy-start.3 = (f32[4,2,2,16,256]{4,3,2,1,0:T(8,128)}, f32[4,2,2,16,256]{4,3,2,1,0:T(8,128)S(1)}, u32[]{:S(2)}) copy-start(f32[4,2,2,16,256]{4,3,2,1,0:T(8,128)S(1)} %collective-permute-done.5.east) | copy-start | bytes 786436
  31.4 4.6 %copy-start.6 = (s32[16]{0:T(128)S(1)}, s32[16]{0:T(128)}, u32[]{:S(2)}) copy-start(s32[16]{0:T(128)} %param.9) | copy-start | bytes 196
  36.0 0.7 copy-start.4
  36.0 0.7 copy-start.5

commit v2 on v1

--- a/solution.py
+++ b/solution.py
@@ -14,6 +14,7 @@
 edge_rows = (0, 1, 6, 7)
 smem = pl.BlockSpec(memory_space=pltpu.SMEM)
 vmem = pl.BlockSpec(memory_space=pltpu.VMEM)
+room = pltpu.CompilerParams(vmem_limit_bytes=16 << 20)
 
 
 def taper_of(distance_sq, radius):
@@ -298,6 +299,7 @@
         ),
         in_specs=[vmem, smem, vmem, smem, vmem, vmem],
         name="interior",
+        compiler_params=room,
     )(state, diffusion, obs_cells, obs_count, obs_value, obs_error)
     edge, winds, grid = pl.pallas_call(
         edge_kernel,
@@ -308,6 +310,7 @@
         ),
         in_specs=[vmem, smem] + [vmem] * 5,
         name="edges",
+        compiler_params=room,
     )(state, diffusion, west_a, east_a, once, column, grids)
     before = lax.ppermute(grid, "space", up)
     after = lax.ppermute(grid, "space", down)
@@ -316,6 +319,7 @@
         out_shape=shape(members, 2, 4, levels, lat_cells),
         in_specs=[vmem, smem] + [vmem] * 6,
         name="edges_rest",
+        compiler_params=room,
     )(state, diffusion, west_a, east_a, west_b, east_b, once, winds)
     sends = pl.pallas_call(
         weights_kernel,
@@ -327,10 +331,11 @@
             pltpu.VMEM((members, len(radii), width, lat_cells), f32),
         ],
         name="weights",
+        compiler_params=room,
     )(level_radius, grid, before, after, inner, edge, rest)
     parts = lax.all_to_all(sends, "mem", 0, 0, tiled=True)
     share = pl.pallas_call(
-        combine_kernel, out_shape=shape(width, 80, lat_cells), in_specs=[vmem] * 2, name="combine"
+        combine_kernel, out_shape=shape(width, 80, lat_cells), in_specs=[vmem] * 2, name="combine", compiler_params=room
     )(level_radius, parts)
     mean = lax.all_to_all(share, "mem", 0, 0, tiled=True)
 
@@ -349,6 +354,7 @@
         ],
         out_specs=per_member(fields, width, levels, lat_cells),
         name="blend",
+        compiler_params=room,
     )(mean, inner, edge, rest)
 
 

time: 78.3 us -> 62.6 us (0.80); the launches traced: 77 us -> 62.5 us
  Pallas kernels: 26.2 us -> 10.7 us
  blocking collectives: 29.3 us -> 32.1 us
  local copies, waits for them, and re-layouts: 4.58 us -> 2.49 us
    pallas_call x1, Pallas kernels: 4.56 us -> 1.51 us  [local(): pl.pallas_call(edge_rest_kernel, out_shape=shape(members, 2, 4, levels, l...]
    pallas_call x1, Pallas kernels: 4.88 us -> 1.93 us  [local(): pl.pallas_call(edge_kernel, out_shape=(shape(members, 3, 4, levels, lat_c...]
    all_to_all x1, blocking collectives: 15.6 us -> 18.4 us  [local(): parts = lax.all_to_all(sends, 'mem', 0, 0, tiled=True)]
    pallas_call x1, Pallas kernels: 5.71 us -> 3.05 us  [local(): pl.pallas_call(interior_kernel, out_shape=(shape(members, fields, 6, leve...]
    pallas_call x1, Pallas kernels: 4.63 us -> 2.03 us  [local(): pl.pallas_call(weights_kernel, out_shape=shape(width, 96, lat_cells), in_...]
    pallas_call x1, Pallas kernels: 4.32 us -> 2.05 us  [local(): pl.pallas_call(blend_kernel, grid=(members,), out_shape=shape(*state.shap...]
    ppermute x1, starting transfers between devices: 0.01 us -> 2.09 us  [local(): before = lax.ppermute(grid, 'space', up)]
    ppermute x1, starting transfers between devices: 5.36 us -> 3.35 us  [local(): after = lax.ppermute(grid, 'space', down)]
  transfers between devices with their start and end apart: 6 -> 6, of which waited for: 0 -> 1; matrix products, arithmetic and copies ran while one was open for 1% -> 2% of each run, Pallas kernels for 20% -> 10%
where the time goes in v2:
time: 62.6 us; the launch traced here: 62.5 us
  blocking collectives  32.1 us (51%)
  starting transfers between devices  16.3 us (26%)
  Pallas kernels  10.7 us (17%)
  local copies, waits for them, and re-layouts  2.49 us (4%)
  between operations  0.8 us (1%)
    all_to_all x1, blocking collectives, local(): parts = lax.all_to_all(sends, 'mem', 0, 0, tiled=True)  18.4 us
    all_to_all x1, blocking collectives, local(): mean = lax.all_to_all(share, 'mem', 0, 0, tiled=True)  13.7 us
    ppermute x1, starting transfers between devices, local(): east_a = lax.ppermute(state[:, :3, 0:2], 'space', down)  5.35 us
    ppermute x1, starting transfers between devices, local(): east_b = lax.ppermute(state[:, 3:, 0:2], 'space', down)  5.35 us
    ppermute x1, starting transfers between devices, local(): after = lax.ppermute(grid, 'space', down)  3.35 us
    pallas_call x1, Pallas kernels, local(): pl.pallas_call(interior_kernel, out_shape=(shape(members, fields, 6, leve...  3.05 us
    ppermute x1, starting transfers between devices, local(): before = lax.ppermute(grid, 'space', up)  2.09 us
    pallas_call x1, Pallas kernels, local(): pl.pallas_call(blend_kernel, grid=(members,), out_shape=shape(*state.shap...  2.05 us
  transfers between devices with their start and end apart: 6, of which 1 were waited for; matrix products, arithmetic and copies ran while one was open for 2% of the time, Pallas kernels for 10%

profile of v2, /device:TPU:128, one launch (start us, length us, event | category | flops | bytes accessed | tf_op | source)
XLA Modules:
  0.0 62.5 jit_solution(9074651511794306548)
XLA Ops:
  0.0 0.0 copy-start
  0.0 0.0 copy-start.4
  0.0 0.0 copy-start.1
  0.0 1.3 %fusion.1 = (f32[4,3,2,16,256]{4,3,2,1,0:T(8,128)S(1)}, f32[4,3,2,16,256]{4,3,2,1,0:T(8,128)S(1)}) fusion(f32[4,5,8,16,256]{4,3,2,1,0:T(8,128)} %state.5), kind=kLoop, calls=%fused_computation.1 | loop fusion | bytes 1572864 | tf_op jit(solution)/shard_map/slice | solution.py:287
  1.4 0.1 collective-permute-start
  1.5 5.3 %collective-permute-start.1 = (f32[4,3,2,16,256]{4,3,2,1,0:T(8,128)S(1)}, f32[4,3,2,16,256]{4,3,2,1,0:T(8,128)S(1)}, u32[]{:S(2)}, u32[]{:S(2)}) collective-permute-start(f32[4,3,2,16,256]{4,3,2,1,0:T(8,128)S(1)} %get-tuple-element.21), channel_id=1, source_target_pairs={{1,0},{2,1},{3,2},{4,3},{5,4},{6,5},{7,6},{8,7},{9,8},{10,9},{11,1... | collective-permute-start | bytes 1179656 | tf_op jit(solution)/shard_map/ppermute | solution.py:287
  6.8 1.1 %fusion = (f32[4,2,2,16,256]{4,3,2,1,0:T(8,128)S(1)}, f32[4,2,2,16,256]{4,3,2,1,0:T(8,128)S(1)}) fusion(f32[4,5,8,16,256]{4,3,2,1,0:T(8,128)} %state.5), kind=kLoop, calls=%fused_computation | loop fusion | bytes 1048576 | tf_op jit(solution)/shard_map/slice | solution.py:289
  7.9 0.1 collective-permute-start.4
  8.0 5.3 %collective-permute-start.5 = (f32[4,2,2,16,256]{4,3,2,1,0:T(8,128)S(1)}, f32[4,2,2,16,256]{4,3,2,1,0:T(8,128)S(1)}, u32[]{:S(2)}, u32[]{:S(2)}) collective-permute-start(f32[4,2,2,16,256]{4,3,2,1,0:T(8,128)S(1)} %get-tuple-element.19), channel_id=1, source_target_pairs={{1,0},{2,1},{3,2},{4,3},{5,4},{6,5},{7,6},{8,7},{9,8},{10,9},{11,1... | collective-permute-start | bytes 786440 | tf_op jit(solution)/shard_map/ppermute | solution.py:289
  14.0 0.0 copy-done
  14.0 0.0 copy-done.2
  14.0 0.0 copy-done.3
  14.0 0.0 copy-done.4
  14.0 0.0 copy-done.1
  14.0 3.0 %interior.1 = (f32[4,5,6,16,256]{4,3,2,1,0:T(8,128)S(1)}, f32[4,5,4,16,256]{4,3,2,1,0:T(8,128)S(1)}, f32[4,4,256]{2,1,0:T(4,128)S(1)}, f32[3,8,256]{2,1,0:T(8,128)S(1)}) custom-call(f32[4,5,8,16,256]{4,3,2,1,0:T(8,128)S(1)} %copy-done, f32[5]{0:T(128)S(1)} %copy-done.1, s32[1,128]{1,0:T(1,128)S(1)} %copy-done.2, s32[1]{0:T(128)S(6)} %copy.8.count, ...), custom_call_target="tpu_custom_call" | custom-call | tf_op jit(solution)/shard_map/interior/pallas_call | solution.py:292
  17.1 0.0 collective-permute-done.west.west_winds
  17.1 0.0 collective-permute-done.1.east.east_winds
  17.1 1.9 %edges.1 = (f32[4,3,4,16,256]{4,3,2,1,0:T(8,128)S(1)}, f32[4,2,4,16,256]{4,3,2,1,0:T(8,128)S(1)}, f32[4,8,256]{2,1,0:T(8,128)S(1)}) custom-call(f32[4,5,8,16,256]{4,3,2,1,0:T(8,128)S(1)} %copy-done, f32[5]{0:T(128)S(1)} %copy-done.1, f32[4,3,2,16,256]{4,3,2,1,0:T(8,128)S(1)} %collective-permute-done.west.west_winds, ...), custom_call_target="tpu_custom_call" | custom-call | tf_op jit(solution)/shard_map/edges/pallas_call | solution.py:304
  19.0 2.1 %collective-permute-start.2 = (f32[4,8,256]{2,1,0:T(8,128)S(1)}, f32[4,8,256]{2,1,0:T(8,128)S(1)}, u32[]{:S(2)}, u32[]{:S(2)}) collective-permute-start(f32[4,8,256]{2,1,0:T(8,128)S(1)} %get-tuple-element.15.own), channel_id=1, source_target_pairs={{0,1},{1,2},{2,3},{3,4},{4,5},{5,6},{6,7},{7,8},{8,9},{9,10},{10,1... | collective-permute-start | bytes 98312 | tf_op jit(solution)/shard_map/ppermute | solution.py:315
  21.1 3.4 %collective-permute-start.3 = (f32[4,8,256]{2,1,0:T(8,128)S(1)}, f32[4,8,256]{2,1,0:T(8,128)S(1)}, u32[]{:S(2)}, u32[]{:S(2)}) collective-permute-start(f32[4,8,256]{2,1,0:T(8,128)S(1)} %get-tuple-element.15.own), channel_id=1, source_target_pairs={{1,0},{2,1},{3,2},{4,3},{5,4},{6,5},{7,6},{8,7},{9,8},{10,9},{11,1... | collective-permute-start | bytes 98312 | tf_op jit(solution)/shard_map/ppermute | solution.py:316
  24.5 0.0 collective-permute-done.4.west
  24.5 0.0 collective-permute-done.5.east
  24.5 1.5 %edges_rest.1.rest = f32[4,2,4,16,256]{4,3,2,1,0:T(8,128)S(1)} custom-call(f32[4,5,8,16,256]{4,3,2,1,0:T(8,128)S(1)} %copy-done, f32[5]{0:T(128)S(1)} %copy-done.1, f32[4,3,2,16,256]{4,3,2,1,0:T(8,128)S(1)} %collective-permute-done.west.west_winds, f32[4,3,2,16,256]{4,3,2,1,0:T(8,128)S(1)} %collective-permute-done.1.east.east_winds, ...), custom_call_target="tpu_custom_call" | custom-call | tf_op jit(solution)/shard_map/edges_rest/pallas_call | solution.py:317
  26.0 0.1 collective-permute-done.2.before
  26.1 0.0 collective-permute-done.3.after
  26.1 0.0 copy-done.5
  26.1 0.1 broadcast_in_dim.2.level_radius
  26.1 2.0 %weights.1 = f32[8,96,256]{2,1,0:T(8,128)S(1)} custom-call(s32[16,256]{1,0:T(8,128)S(1)} %broadcast_in_dim.2.level_radius, f32[4,8,256]{2,1,0:T(8,128)S(1)} %get-tuple-element.15.own, f32[4,8,256]{2,1,0:T(8,128)S(1)} %collective-permute-done.2.before, f32[4,8,256]{2,1,0:T(8,128)S(1)} %collective-permute-done.3.after, ...), custom_call_target="tpu_custom_call" | custom-call | tf_op jit(solution)/shard_map/weights/pallas_call | solution.py:324
  28.2 18.4 %all_to_all.10.parts = f32[8,96,256]{2,1,0:T(8,128)S(1)} all-to-all(f32[8,96,256]{2,1,0:T(8,128)S(1)} %weights.1), channel_id=1, replica_groups=mesh['mem'=8,'space'=32] {'mem'}, dimensions={0} | all-to-all | bytes 1572864 | tf_op jit(solution)/shard_map/all_to_all | solution.py:336
  46.6 0.1 combine.1
  46.7 13.7 %all_to_all.11.mean = f32[8,80,256]{2,1,0:T(8,128)S(1)} all-to-all(f32[8,80,256]{2,1,0:T(8,128)S(1)} %combine.1), channel_id=1, replica_groups=mesh['mem'=8,'space'=32] {'mem'}, dimensions={0} | all-to-all | bytes 1310720 | tf_op jit(solution)/shard_map/all_to_all | solution.py:340
  60.4 2.0 %blend.1 = f32[4,5,8,16,256]{4,3,2,1,0:T(8,128)} custom-call(f32[8,80,256]{2,1,0:T(8,128)S(1)} %all_to_all.11.mean, f32[4,5,4,16,256]{4,3,2,1,0:T(8,128)S(1)} %get-tuple-element.16.inner, f32[4,3,4,16,256]{4,3,2,1,0:T(8,128)S(1)} %get-tuple-element.17.edge, f32[4,2,4,16,256]{4,3,2,1,0:T(8,128)S(1)} %edges_rest.1.rest), custom_call_target="tpu_custom_call" | custom-call | tf_op jit(solution)/shard_map/blend/pallas_call | solution.py:345
  (3 shorter events, 0.0 us)
Async XLA Ops:
  0.0 14.0 %copy-start = (f32[4,5,8,16,256]{4,3,2,1,0:T(8,128)S(1)}, f32[4,5,8,16,256]{4,3,2,1,0:T(8,128)}, u32[]{:S(2)}) copy-start(f32[4,5,8,16,256]{4,3,2,1,0:T(8,128)} %state.5) | copy-start | bytes 7864324
  0.0 14.0 %copy-start.2 = (s32[1,128]{1,0:T(1,128)S(1)}, s32[1,128]{1,0:T(1,128)}, u32[]{:S(2)}) copy-start(s32[1,128]{1,0:T(1,128)} %cells.1) | copy-start | bytes 1540
  0.0 14.0 %copy-start.3 = (f32[1,128]{1,0:T(1,128)S(1)}, f32[1,128]{1,0:T(1,128)}, u32[]{:S(2)}) copy-start(f32[1,128]{1,0:T(1,128)} %value.1) | copy-start | bytes 1540
  0.0 14.0 %copy-start.4 = (f32[1,128]{1,0:T(1,128)S(1)}, f32[1,128]{1,0:T(1,128)}, u32[]{:S(2)}) copy-start(f32[1,128]{1,0:T(1,128)} %error.1) | copy-start | bytes 1540
  0.0 14.0 %copy-start.1 = (f32[5]{0:T(128)S(1)}, f32[5]{0:T(128)}, u32[]{:S(2)}) copy-start(f32[5]{0:T(128)} %diffusion.5) | copy-start | bytes 64
  1.4 15.7 %collective-permute-start = (f32[4,3,2,16,256]{4,3,2,1,0:T(8,128)S(1)}, f32[4,3,2,16,256]{4,3,2,1,0:T(8,128)S(1)}, u32[]{:S(2)}, u32[]{:S(2)}) collective-permute-start(f32[4,3,2,16,256]{4,3,2,1,0:T(8,128)S(1)} %get-tuple-element.22), channel_id=1, source_target_pairs={{0,1},{1,2},{2,3},{3,4},{4,5},{5,6},{6,7},{7,8},{8,9},{9,10},{10,1... | collective-permute-start | bytes 1179656 | tf_op jit(solution)/shard_map/ppermute | solution.py:286
  1.5 15.6 %collective-permute-start.1 = (f32[4,3,2,16,256]{4,3,2,1,0:T(8,128)S(1)}, f32[4,3,2,16,256]{4,3,2,1,0:T(8,128)S(1)}, u32[]{:S(2)}, u32[]{:S(2)}) collective-permute-start(f32[4,3,2,16,256]{4,3,2,1,0:T(8,128)S(1)} %get-tuple-element.21), channel_id=1, source_target_pairs={{1,0},{2,1},{3,2},{4,3},{5,4},{6,5},{7,6},{8,7},{9,8},{10,9},{11,1... | collective-permute-start | bytes 1179656 | tf_op jit(solution)/shard_map/ppermute | solution.py:287
  7.9 16.6 %collective-permute-start.4 = (f32[4,2,2,16,256]{4,3,2,1,0:T(8,128)S(1)}, f32[4,2,2,16,256]{4,3,2,1,0:T(8,128)S(1)}, u32[]{:S(2)}, u32[]{:S(2)}) collective-permute-start(f32[4,2,2,16,256]{4,3,2,1,0:T(8,128)S(1)} %get-tuple-element.20), channel_id=1, source_target_pairs={{0,1},{1,2},{2,3},{3,4},{4,5},{5,6},{6,7},{7,8},{8,9},{9,10},{10,1... | collective-permute-start | bytes 786440 | tf_op jit(solution)/shard_map/ppermute | solution.py:288
  8.0 16.5 %collective-permute-start.5 = (f32[4,2,2,16,256]{4,3,2,1,0:T(8,128)S(1)}, f32[4,2,2,16,256]{4,3,2,1,0:T(8,128)S(1)}, u32[]{:S(2)}, u32[]{:S(2)}) collective-permute-start(f32[4,2,2,16,256]{4,3,2,1,0:T(8,128)S(1)} %get-tuple-element.19), channel_id=1, source_target_pairs={{1,0},{2,1},{3,2},{4,3},{5,4},{6,5},{7,6},{8,7},{9,8},{10,9},{11,1... | collective-permute-start | bytes 786440 | tf_op jit(solution)/shard_map/ppermute | solution.py:289
  19.0 7.0 %collective-permute-start.2 = (f32[4,8,256]{2,1,0:T(8,128)S(1)}, f32[4,8,256]{2,1,0:T(8,128)S(1)}, u32[]{:S(2)}, u32[]{:S(2)}) collective-permute-start(f32[4,8,256]{2,1,0:T(8,128)S(1)} %get-tuple-element.15.own), channel_id=1, source_target_pairs={{0,1},{1,2},{2,3},{3,4},{4,5},{5,6},{6,7},{7,8},{8,9},{9,10},{10,1... | collective-permute-start | bytes 98312 | tf_op jit(solution)/shard_map/ppermute | solution.py:315
  21.1 4.9 %collective-permute-start.3 = (f32[4,8,256]{2,1,0:T(8,128)S(1)}, f32[4,8,256]{2,1,0:T(8,128)S(1)}, u32[]{:S(2)}, u32[]{:S(2)}) collective-permute-start(f32[4,8,256]{2,1,0:T(8,128)S(1)} %get-tuple-element.15.own), channel_id=1, source_target_pairs={{1,0},{2,1},{3,2},{4,3},{5,4},{6,5},{7,6},{8,7},{9,8},{10,9},{11,1... | collective-permute-start | bytes 98312 | tf_op jit(solution)/shard_map/ppermute | solution.py:316
  24.5 1.6 %copy-start.5 = (s32[16]{0:T(128)S(1)}, s32[16]{0:T(128)}, u32[]{:S(2)}) copy-start(s32[16]{0:T(128)} %param.9) | copy-start | bytes 196

commit v3 on v2

v3 whole, which is shorter than its diff:
```python
import jax
import jax.numpy as jnp
import numpy as np
from jax import lax
from jax.experimental import pallas as pl
from jax.experimental.pallas import tpu as pltpu
from jax.sharding import PartitionSpec as P

time_step = 0.2
blend_share = 0.5
radii = (4, 5, 6, 7, 8)
reach = 7
f32 = jnp.float32
anywhere = pl.BlockSpec(memory_space=pl.ANY)
smem = pl.BlockSpec(memory_space=pltpu.SMEM)
vmem = pl.BlockSpec(memory_space=pltpu.VMEM)
room = pltpu.CompilerParams(vmem_limit_bytes=16 << 20)


def taper_of(distance_sq, radius):
    inverse = np.float32(1.0) / np.float32(radius * radius)
    share = max(np.float32(0.0), np.float32(1.0) - np.float32(distance_sq) * inverse)
    return float(np.float32(share * share))


def step_row(centre, west, east, u_part, v_part, rate):
    size = centre.shape[-1]
    north = pltpu.roll(centre, size - 1, 1)
    south = pltpu.roll(centre, 1, 1)
    spread = (east + west) + (north + south) - 4.0 * centre
    return centre + (rate * spread - (u_part * (east - west) + v_part * (north - south)))


def natural(row, parity):
    return row + parity * (7 - 2 * row)


def step_inner(centre, inner, u_part, v_part, rate):
    size = centre.shape[-1]
    north = pltpu.roll(centre, size - 1, 1)
    south = pltpu.roll(centre, 1, 1)
    spread = inner + (north + south) - 4.0 * centre
    return centre + (rate * spread - (u_part * inner + v_part * (north - south)))


def interior_kernel(
    parity_ref, state, near, diffusion, radius, cells, count, value, error,
    core, once_one, pre_zero, pre_one, column, grids, level_radius, far, once,
):
    sites = cells.shape[1]
    lat_cells = state.shape[4]
    parity = parity_ref[0]
    half = 0.5 * time_step
    signed = half * (1 - 2 * parity).astype(f32)
    far_start = 6 * parity

    def member(m, carry):
        def at(f, k):
            if k < 8:
                return state[m, f, natural(k, parity)]
            return near[m, f, parity if k == 8 else 1 - parity]

        for k in range(1, 9):
            u_part, v_part = signed * at(0, k), half * at(1, k)
            for f in range(5):
                once[f, k - 1] = step_row(
                    at(f, k), at(f, k - 1), at(f, k + 1), u_part, v_part, diffusion[f] * time_step
                )
        u_part, v_part = signed * at(0, 0), half * at(1, 0)
        for f in range(5):
            pre_zero[m, f] = step_inner(at(f, 0), at(f, 1), u_part, v_part, diffusion[f] * time_step)
        u_part, v_part = signed * once[0, 0], half * once[1, 0]
        for f in range(5):
            pre_one[m, f] = step_inner(once[f, 0], once[f, 1], u_part, v_part, diffusion[f] * time_step)
            once_one[m, f] = once[f, 0]
        column[m] = jnp.zeros((8, lat_cells), f32)
        for k in range(2, 8):
            u_part, v_part = signed * once[0, k - 1], half * once[1, k - 1]
            for f in range(5):
                row = step_row(
                    once[f, k - 1], once[f, k - 2], once[f, k], u_part, v_part, diffusion[f] * time_step
                )
                core[m, f, k - 2] = row
                if f == 2:
                    column[m, pl.ds(natural(k, parity), 1)] = jnp.mean(row, axis=0, keepdims=True)
        for f in (3, 4):
            for k in range(2):
                far[m, f - 3, k] = state[m, f, far_start + k]
        return carry

    lax.fori_loop(0, state.shape[0], member, 0)

    cell = cells[...]
    site_x = cell // lat_cells
    site_y = cell % lat_cells
    valid = lax.broadcasted_iota(jnp.int32, (1, sites), 1) < count[0]
    weight = jnp.where(valid, 1.0 / (error[...] * error[...]), 0.0)
    moments = jnp.concatenate([weight, weight * value[...], weight * value[...] * value[...]], axis=0)
    at_x = lax.broadcasted_iota(jnp.int32, (8, sites), 0) == site_x
    at_y = (lax.broadcasted_iota(jnp.int32, (lat_cells, sites), 0) == site_y).astype(f32)
    stacked = jnp.concatenate(
        [jnp.where(at_x, moments[k : k + 1], 0.0) for k in range(3)], axis=0
    )
    sums = lax.dot_general(
        stacked, at_y, (((1,), (1,)), ((), ())), precision=lax.Precision.HIGHEST, preferred_element_type=f32
    )
    total, first, second = sums[0:8], sums[8:16], sums[16:24]
    mean = jnp.where(total > 0.0, first / jnp.where(total > 0.0, total, 1.0), 0.0)
    grids[0] = total
    grids[1] = mean
    grids[2] = second - first * mean
    levels = level_radius.shape[0]
    level = lax.broadcasted_iota(jnp.int32, (levels, lat_cells), 0)
    chosen = jnp.full((levels, lat_cells), radius[0], jnp.int32)
    for z in range(1, levels):
        chosen = jnp.where(level == z, radius[z], chosen)
    level_radius[...] = chosen


def far_rows(beyond, next_to, zero, once_one, pre_zero, pre_one, winds, rate):
    (u_beyond, v_beyond), (u_zero, _), (u_one, _) = winds
    outside = step_row(next_to, beyond, zero, u_beyond, v_beyond, rate)
    first = pre_zero + next_to * (rate + u_zero)

    def again(u_part, v_part):
        return (
            step_row(first, outside, once_one, u_part, v_part, rate),
            pre_one + first * (rate + u_one),
        )

    return first, again


def far_winds(m, parity, state, far, once_one):
    half = 0.5 * time_step
    signed = half * (1 - 2 * parity).astype(f32)
    row = natural(0, parity)
    return (
        (signed * far[m, 0, 1 - parity], half * far[m, 1, 1 - parity]),
        (signed * state[m, 0, row], None),
        (signed * once_one[m, 0], None),
    )


def far_kernel(
    parity_ref, state, diffusion, far, once_one, pre_zero, pre_one, column, grids, edge, winds_out, grid, full
):
    parity = parity_ref[0]
    half = 0.5 * time_step
    signed = half * (1 - 2 * parity).astype(f32)

    def member(m, carry):
        winds = far_winds(m, parity, state, far, once_one)
        pairs = [
            far_rows(
                far[m, f, parity], far[m, f, 1 - parity], state[m, f, natural(0, parity)],
                once_one[m, f], pre_zero[m, f], pre_one[m, f], winds, diffusion[f] * time_step,
            )
            for f in range(3)
        ]
        u_part, v_part = signed * pairs[0][0], half * pairs[1][0]
        winds_out[m, 0] = u_part
        winds_out[m, 1] = v_part
        full[m] = column[m]
        for f in (2, 0, 1):
            for k, row in enumerate(pairs[f][1](u_part, v_part)):
                edge[m, f, k] = row
                if f == 2:
                    full[m, pl.ds(natural(k, parity), 1)] = jnp.mean(row, axis=0, keepdims=True)
        off = full[m] - grids[1]
        grid[m] = grids[0] * (off * off) + grids[2]
        return carry

    lax.fori_loop(0, state.shape[0], member, 0, unroll=True)


def far_rest_kernel(parity_ref, state, diffusion, far_winds_ref, far, once_one, pre_zero, pre_one, winds_in, edge):
    parity = parity_ref[0]

    def member(m, carry):
        winds = far_winds(m, parity, state, far_winds_ref, once_one)
        for f in (3, 4):
            _, again = far_rows(
                far[m, f - 3, parity], far[m, f - 3, 1 - parity], state[m, f, natural(0, parity)],
                once_one[m, f], pre_zero[m, f], pre_one[m, f], winds, diffusion[f] * time_step,
            )
            for k, row in enumerate(again(winds_in[m, 0], winds_in[m, 1])):
                edge[m, f - 3, k] = row
        return carry

    lax.fori_loop(0, state.shape[0], member, 0, unroll=True)


def by_level(rows, level_radius):
    result = jnp.broadcast_to(rows[0], level_radius.shape)
    for k in range(1, len(radii)):
        result = jnp.where(level_radius == radii[k], rows[k], result)
    return result


def final_row(m, f, k, core, edge, rest):
    if k >= 2:
        return core[m, f, k - 2]
    return edge[m, f, k] if f < 3 else rest[m, f - 3, k]


def weights_kernel(parity_ref, level_radius, own, beside, beyond, core, edge, rest, sends, near, shifted, expo):
    members, width, lat_cells = own.shape
    half = lat_cells // 2
    parity = parity_ref[0]

    def convolve(m, carry):
        near[m, pl.ds(16 * parity, 8)] = beyond[m]
        near[m, 8:16] = own[m]
        near[m, pl.ds(16 * (1 - parity), 8)] = beside[m]
        grid = near[m]
        for h in range(2):
            shifted[m, 0, h] = grid[:, half * h : half * h + half]
        for dy in range(1, reach + 1):
            both = pltpu.roll(grid, dy, 1) + pltpu.roll(grid, lat_cells - dy, 1)
            for h in range(2):
                shifted[m, dy, h] = both[:, half * h : half * h + half]
        for h in range(2):
            sums = [None] * len(radii)
            for dx in range(reach + 1):
                for dy in range(reach + 1):
                    distance_sq = dx * dx + dy * dy
                    if distance_sq >= radii[-1] ** 2:
                        continue
                    if dx == 0:
                        pair = shifted[m, dy, h, 8:16]
                    else:
                        pair = shifted[m, dy, h, 8 + dx : 16 + dx] + shifted[m, dy, h, 8 - dx : 16 - dx]
                    for k, radius in enumerate(radii):
                        if distance_sq < radius * radius:
                            term = pair * (-0.5 * taper_of(distance_sq, radius))
                            sums[k] = term if sums[k] is None else sums[k] + term
            for k in range(len(radii)):
                expo[m, k, :, half * h : half * h + half] = sums[k]
        return carry

    lax.fori_loop(0, members, convolve, 0, unroll=True)
    for k in range(len(radii)):
        logs = [expo[m, k] for m in range(members)]
        best = logs[0]
        for m in range(1, members):
            best = jnp.maximum(best, logs[m])
        values = [jnp.exp(logs[m] - best) for m in range(members)]
        total = values[0]
        for m in range(1, members):
            total = total + values[m]
        over = 1.0 / total
        for m in range(members):
            expo[m, k] = values[m] * over
        level_log = best + jnp.log(total)
        for x in range(width):
            sends[natural(x, parity), 80 + k : 81 + k] = level_log[x : x + 1]
    for x in range(width):
        here = pl.ds(natural(x, parity), 1)
        sends[x, 85:88] = jnp.zeros((3, lat_cells), f32)
        sums = [None] * 5
        for m in range(members):
            weight = by_level([expo[m, k, here] for k in range(len(radii))], level_radius[...])
            for f in range(5):
                row = final_row(m, f, x, core, edge, rest)
                term = weight * row
                sums[f] = term if sums[f] is None else sums[f] + term
        for f in range(5):
            sends[x, 16 * f : 16 * f + 16] = sums[f]


def combine_kernel(level_radius, parts, result):
    sources = parts.shape[0]
    logs = [parts[d, 80:85] for d in range(sources)]
    best = logs[0]
    for d in range(1, sources):
        best = jnp.maximum(best, logs[d])
    scales = [jnp.exp(logs[d] - best) for d in range(sources)]
    total = scales[0]
    for d in range(1, sources):
        total = total + scales[d]
    over = 1.0 / total
    sums = [None] * 5
    for d in range(sources):
        share = scales[d] * over
        weight = by_level([share[k : k + 1] for k in range(len(radii))], level_radius[...])
        for f in range(5):
            term = weight * parts[d, 16 * f : 16 * f + 16]
            sums[f] = term if sums[f] is None else sums[f] + term
    for f in range(5):
        for d in range(sources):
            result[d, 16 * f : 16 * f + 16] = sums[f]


def blend_kernel(parity_ref, mean, core, edge, rest, out, done, sems):
    members = core.shape[0]
    parity = parity_ref[0]
    copies = []
    for m in range(members):
        for part in range(2):
            for k in range(4 * part, 4 * part + 4):
                for f in range(5):
                    row = final_row(m, f, k, core, edge, rest)
                    done[m, f, natural(k, parity)] = row + blend_share * (mean[k, 16 * f : 16 * f + 16] - row)
            rows = pl.ds(4 * (part + parity * (1 - 2 * part)), 4)
            copy = pltpu.make_async_copy(done.at[m, :, rows], out.at[m, :, rows], sems.at[m, part])
            copy.start()
            copies.append(copy)
    for copy in copies:
        copy.wait()


def local(state, diffusion, radius, obs_cells, obs_count, obs_value, obs_error):
    members, fields, width, levels, lat_cells = state.shape
    size = lax.axis_size("space")
    parity = (lax.axis_index("space") & 1).astype(jnp.int32).reshape(1)
    beside_pairs = [(i, i + 1 - 2 * (i % 2)) for i in range(size)]
    beyond_pairs = [(i, (i - 1 + 2 * (i % 2)) % size) for i in range(size)]

    def shape(*dims):
        return jax.ShapeDtypeStruct(dims, f32)

    near = lax.dynamic_slice_in_dim(state, 6 * (1 - parity[0]), 2, axis=2)
    far_a = lax.dynamic_slice_in_dim(state[:, :3], 6 * parity[0], 2, axis=2)
    near = lax.ppermute(near, "space", beside_pairs)
    far_a = lax.ppermute(far_a, "space", beyond_pairs)
    core, once_one, pre_zero, pre_one, column, grids, level_radius, far_b = pl.pallas_call(
        interior_kernel,
        out_shape=(
            shape(members, fields, 6, levels, lat_cells),
            shape(members, fields, levels, lat_cells),
            shape(members, fields, levels, lat_cells),
            shape(members, fields, levels, lat_cells),
            shape(members, width, lat_cells),
            shape(3, width, lat_cells),
            jax.ShapeDtypeStruct((levels, lat_cells), jnp.int32),
            shape(members, 2, 2, levels, lat_cells),
        ),
        in_specs=[smem, vmem, vmem, smem, smem, vmem, smem, vmem, vmem],
        scratch_shapes=[pltpu.VMEM((fields, 8, levels, lat_cells), f32)],
        name="interior",
        compiler_params=room,
    )(parity, state, near, diffusion, radius, obs_cells, obs_count, obs_value, obs_error)
    far_b = lax.ppermute(far_b, "space", beyond_pairs)
    edge, winds, grid = pl.pallas_call(
        far_kernel,
        out_shape=(
            shape(members, 3, 2, levels, lat_cells),
            shape(members, 2, levels, lat_cells),
            shape(members, width, lat_cells),
        ),
        in_specs=[smem, vmem, smem] + [vmem] * 6,
        scratch_shapes=[pltpu.VMEM((members, width, lat_cells), f32)],
        name="edges",
        compiler_params=room,
    )(parity, state, diffusion, far_a, once_one, pre_zero, pre_one, column, grids)
    beside = lax.ppermute(grid, "space", beside_pairs)
    beyond = lax.ppermute(grid, "space", beyond_pairs)
    rest = pl.pallas_call(
        far_rest_kernel,
        out_shape=shape(members, 2, 2, levels, lat_cells),
        in_specs=[smem, vmem, smem] + [vmem] * 6,
        name="edges_rest",
        compiler_params=room,
    )(parity, state, diffusion, far_a, far_b, once_one, pre_zero, pre_one, winds)
    sends = pl.pallas_call(
        weights_kernel,
        out_shape=shape(width, 88, lat_cells),
        in_specs=[smem] + [vmem] * 7,
        scratch_shapes=[
            pltpu.VMEM((members, 24, lat_cells), f32),
            pltpu.VMEM((members, reach + 1, 2, 24, lat_cells // 2), f32),
            pltpu.VMEM((members, len(radii), width, lat_cells), f32),
        ],
        name="weights",
        compiler_params=room,
    )(parity, level_radius, grid, beside, beyond, core, edge, rest)
    parts = lax.all_to_all(sends, "mem", 0, 0, tiled=True)
    share = pl.pallas_call(
        combine_kernel,
        out_shape=shape(width, 80, lat_cells),
        in_specs=[vmem] * 2,
        name="combine",
        compiler_params=room,
    )(level_radius, parts)
    mean = lax.all_to_all(share, "mem", 0, 0, tiled=True)
    return pl.pallas_call(
        blend_kernel,
        out_shape=shape(*state.shape),
        in_specs=[smem] + [vmem] * 4,
        out_specs=anywhere,
        scratch_shapes=[pltpu.VMEM(state.shape, f32), pltpu.SemaphoreType.DMA((members, 2))],
        name="blend",
        compiler_params=room,
    )(parity, mean, core, edge, rest)


def solution(mesh):
    return jax.shard_map(
        local,
        mesh=mesh,
        in_specs=(
            P("mem", None, "space", None, None),
            P(),
            P(),
            P("space", None),
            P("space"),
            P("space", None),
            P("space", None),
        ),
        out_specs=P("mem", None, "space", None, None),
        check_vma=False,
    )
```

time: 62.6 us -> 57 us (0.911); the launches traced: 62.5 us -> 56.1 us
  starting transfers between devices: 16.3 us -> 9.47 us
  waiting for transfers between devices: 0.08 us -> 2.54 us
  Pallas kernels: 10.7 us -> 8.71 us
  local copies, waits for them, and re-layouts: 2.49 us -> 3.24 us
  blocking collectives: 32.1 us -> 31.4 us
    ppermute x6 -> x5, starting transfers between devices: 16.3 us -> 9.47 us  [the longest x1 2.99 us: local(): far_b = lax.ppermute(far_b, 'space', beyond_pairs)]
    pallas_call x4, Pallas kernels: 7.52 us -> 4.2 us  [the longest x1 1.59 us: local(): pl.pallas_call(blend_kernel, out_shape=shape(*state.shape), in_specs=[sme...]
    ppermute x6 -> x5, waiting for transfers between devices: 0.08 us -> 2.54 us  [the longest x1 1.87 us: local(): far_b = lax.ppermute(far_b, 'space', beyond_pairs)]
    slice x2, local copies, waits for them, and re-layouts: 2.4 us -> 0.21 us  [local(): far_a = lax.dynamic_slice_in_dim(state[:, :3], 6 * parity[0], 2, axis=2)]
    unnamed x12, local copies, waits for them, and re-layouts: 0.02 us -> 1.76 us
    pallas_call x1, Pallas kernels: 3.05 us -> 4.39 us  [local(): pl.pallas_call(interior_kernel, out_shape=(shape(members, fields, 6, leve...]
    dynamic_slice x0 -> x2, local copies, waits for them, and re-layouts: none -> 1.28 us  [the longest x1 1.25 us: local(): near = lax.dynamic_slice_in_dim(state, 6 * (1 - parity[0]), 2, axis=2)]
    all_to_all x1, blocking collectives: 18.4 us -> 17.6 us  [local(): parts = lax.all_to_all(sends, 'mem', 0, 0, tiled=True)]
  transfers between devices with their start and end apart: 6 -> 5, of which waited for: 1 -> 2; matrix products, arithmetic and copies ran while one was open for 2% -> 0% of each run, Pallas kernels for 10% -> 11%
where the time goes in v3:
time: 57 us; the launch traced here: 56.1 us
  blocking collectives  31.4 us (55%)
  starting transfers between devices  9.47 us (17%)
  Pallas kernels  8.71 us (15%)
  local copies, waits for them, and re-layouts  3.24 us (6%)
  waiting for transfers between devices  2.54 us (4%)
  between operations  0.8 us (1%)
    all_to_all x1, blocking collectives, local(): parts = lax.all_to_all(sends, 'mem', 0, 0, tiled=True)  17.6 us
    all_to_all x1, blocking collectives, local(): mean = lax.all_to_all(share, 'mem', 0, 0, tiled=True)  13.7 us
    pallas_call x1, Pallas kernels, local(): pl.pallas_call(interior_kernel, out_shape=(shape(members, fields, 6, leve...  4.39 us
    ppermute x1, starting transfers between devices, local(): far_b = lax.ppermute(far_b, 'space', beyond_pairs)  2.99 us
    ppermute x1, starting transfers between devices, local(): far_a = lax.ppermute(far_a, 'space', beyond_pairs)  2.55 us
    ppermute x1, starting transfers between devices, local(): beyond = lax.ppermute(grid, 'space', beyond_pairs)  2.55 us
    ppermute x1, waiting for transfers between devices, local(): far_b = lax.ppermute(far_b, 'space', beyond_pairs)  1.87 us
    unnamed x12, local copies, waits for them, and re-layouts  1.76 us
  transfers between devices with their start and end apart: 5, of which 2 were waited for; matrix products, arithmetic and copies ran while one was open for 0% of the time, Pallas kernels for 11%

profile of v3, /device:TPU:128, one launch (start us, length us, event | category | flops | bytes accessed | tf_op | source)
XLA Modules:
  0.0 56.1 jit_solution(7223410061052165011)
XLA Ops:
  0.0 0.0 slice-start
  0.0 0.0 copy-start.1
  0.0 0.0 copy-start.3
  0.0 0.0 copy-start.4
  0.0 0.0 copy-start.5
  0.0 1.3 %constant_dynamic-slice_fusion.1 = f32[4,5,2,16,256]{4,3,2,1,0:T(8,128)S(1)} fusion(f32[4,5,8,16,256]{4,3,2,1,0:T(8,128)} %state.5, s32[]{:T(128)S(6)} %select_n.6), kind=kLoop, calls=%fused_computation.1 | loop fusion | bytes 1310724 | tf_op jit(solution)/shard_map/dynamic_slice | solution.py:323
  1.3 0.1 collective-permute-start
  1.4 0.2 slice-done
  1.6 2.5 %collective-permute-start.1 = (f32[4,3,2,16,256]{4,3,2,1,0:T(8,128)S(1)}, f32[4,3,2,16,256]{4,3,2,1,0:T(8,128)S(1)}, u32[]{:S(2)}, u32[]{:S(2)}) collective-permute-start(f32[4,3,2,16,256]{4,3,2,1,0:T(8,128)S(1)} %constant_dynamic-slice_fusion), channel_id=1, source_target_pairs={{0,31},{1,2},{2,1},{3,4},{4,3},{5,6},{6,5},{7,8},{8,7},{9,10},{10,... | collective-permute-start | bytes 1179656 | tf_op jit(solution)/shard_map/ppermute | solution.py:326
  4.8 0.0 collective-permute-done.near
  4.8 0.0 copy-done.1
  4.9 0.0 copy-done.2
  4.9 0.0 copy-done.3
  4.9 0.0 copy-done.4
  4.9 0.0 copy-done.5
  4.9 0.0 copy-start
  4.9 1.7 %copy-done = f32[4,5,8,16,256]{4,3,2,1,0:T(8,128)S(1)} copy-done((f32[4,5,8,16,256]{4,3,2,1,0:T(8,128)S(1)}, f32[4,5,8,16,256]{4,3,2,1,0:T(8,128)}, u32[]{:S(2)}) %copy-start) | copy-done | bytes 2621464
  6.6 4.4 %interior.1 = (f32[4,5,6,16,256]{4,3,2,1,0:T(8,128)S(1)}, f32[4,5,16,256]{3,2,1,0:T(8,128)S(1)}, f32[4,5,16,256]{3,2,1,0:T(8,128)S(1)}, f32[4,5,16,256]{3,2,1,0:...) custom-call(s32[1]{0:T(128)} %bitcast.parity_ref, ...), custom_call_target="tpu_custom_call" | custom-call | tf_op jit(solution)/shard_map/interior/pallas_call | solution.py:327
  11.0 3.0 %collective-permute-start.4 = (f32[4,2,2,16,256]{4,3,2,1,0:T(8,128)S(1)}, f32[4,2,2,16,256]{4,3,2,1,0:T(8,128)S(1)}, u32[]{:S(2)}, u32[]{:S(2)}) collective-permute-start(f32[4,2,2,16,256]{4,3,2,1,0:T(8,128)S(1)} %get-tuple-element.25), channel_id=1, source_target_pairs={{0,31},{1,2},{2,1},{3,4},{4,3},{5,6},{6,5},{7,8},{8,7},{9,10},{10,... | collective-permute-start | bytes 786440 | tf_op jit(solution)/shard_map/ppermute | solution.py:344
  14.0 0.0 collective-permute-done.1.far.far_winds_ref
  14.0 0.9 %edges.1 = (f32[4,3,2,16,256]{4,3,2,1,0:T(8,128)S(1)}, f32[4,2,16,256]{3,2,1,0:T(8,128)S(1)}, f32[4,8,256]{2,1,0:T(8,128)S(1)}) custom-call(s32[1]{0:T(128)} %bitcast.parity_ref, f32[4,5,8,16,256]{4,3,2,1,0:T(8,128)S(1)} %copy-done, f32[5]{0:T(128)S(1)} %copy-done.1, f32[4,3,2,16,256]{4,3,2,1,0:T(8,128)S(1)} %collective-permute-done.1.far.far_winds_ref, ...), custom_call_target="tpu_custom_call" | custom-call | tf_op jit(solution)/shard_map/edges/pallas_call | solution.py:345
  14.9 2.5 %collective-permute-start.3 = (f32[4,8,256]{2,1,0:T(8,128)S(1)}, f32[4,8,256]{2,1,0:T(8,128)S(1)}, u32[]{:S(2)}, u32[]{:S(2)}) collective-permute-start(f32[4,8,256]{2,1,0:T(8,128)S(1)} %get-tuple-element.22.own), channel_id=1, source_target_pairs={{0,31},{1,2},{2,1},{3,4},{4,3},{5,6},{6,5},{7,8},{8,7},{9,10},{10,... | collective-permute-start | bytes 98312 | tf_op jit(solution)/shard_map/ppermute | solution.py:358
  17.5 1.3 %collective-permute-start.2 = (f32[4,8,256]{2,1,0:T(8,128)S(1)}, f32[4,8,256]{2,1,0:T(8,128)S(1)}, u32[]{:S(2)}, u32[]{:S(2)}) collective-permute-start(f32[4,8,256]{2,1,0:T(8,128)S(1)} %get-tuple-element.22.own), channel_id=1, source_target_pairs={{0,1},{1,0},{2,3},{3,2},{4,5},{5,4},{6,7},{7,6},{8,9},{9,8},{10,11... | collective-permute-start | bytes 98312 | tf_op jit(solution)/shard_map/ppermute | solution.py:357
  18.8 1.9 %collective-permute-done.4.far = f32[4,2,2,16,256]{4,3,2,1,0:T(8,128)S(1)} collective-permute-done((f32[4,2,2,16,256]{4,3,2,1,0:T(8,128)S(1)}, f32[4,2,2,16,256]{4,3,2,1,0:T(8,128)S(1)}, u32[]{:S(2)}, u32[]{:S(2)}) %collective-permute-start.4) | collective-permute-done | bytes 262176 | tf_op jit(solution)/shard_map/ppermute | solution.py:344
  20.6 0.8 %edges_rest.1.rest = f32[4,2,2,16,256]{4,3,2,1,0:T(8,128)S(1)} custom-call(s32[1]{0:T(128)} %bitcast.parity_ref, f32[4,5,8,16,256]{4,3,2,1,0:T(8,128)S(1)} %copy-done, f32[5]{0:T(128)S(1)} %copy-done.1, f32[4,3,2,16,256]{4,3,2,1,0:T(8,128)S(1)} %collective-permute-done.1.far.far_winds_ref, f32[4,2,2,16,256]{4,3,2,1,0:T(8,128)S(1)} %collective-permute-done.4.far, ...), custom_call_target="tpu_custom_call" | custom-call | tf_op jit(solution)/shard_map/edges_rest/pallas_call | solution.py:359
  21.4 0.7 %collective-permute-done.3.beyond = f32[4,8,256]{2,1,0:T(8,128)S(1)} collective-permute-done((f32[4,8,256]{2,1,0:T(8,128)S(1)}, f32[4,8,256]{2,1,0:T(8,128)S(1)}, u32[]{:S(2)}, u32[]{:S(2)}) %collective-permute-start.3) | collective-permute-done | bytes 32800 | tf_op jit(solution)/shard_map/ppermute | solution.py:358
  22.1 0.0 collective-permute-done.2.beside
  22.1 1.0 %weights.1 = f32[8,88,256]{2,1,0:T(8,128)S(1)} custom-call(s32[1]{0:T(128)} %bitcast.parity_ref, s32[16,256]{1,0:T(8,128)S(1)} %get-tuple-element.16.level_radius, f32[4,8,256]{2,1,0:T(8,128)S(1)} %get-tuple-element.22.own, f32[4,8,256]{2,1,0:T(8,128)S(1)} %collective-permute-done.2.beside, f32[4,8,256]{2,1,0:T(8,128)S(1)} %collective-permute-done.3.beyond, ...), custom_call_target="tpu_custom_call" | custom-call | tf_op jit(solution)/shard_map/weights/pallas_call | solution.py:366
  23.0 17.6 %all_to_all.10.parts = f32[8,88,256]{2,1,0:T(8,128)S(1)} all-to-all(f32[8,88,256]{2,1,0:T(8,128)S(1)} %weights.1), channel_id=1, replica_groups=mesh['mem'=8,'space'=32] {'mem'}, dimensions={0} | all-to-all | bytes 1441792 | tf_op jit(solution)/shard_map/all_to_all | solution.py:378
  40.7 0.1 combine.1
  40.8 13.7 %all_to_all.11.mean = f32[8,80,256]{2,1,0:T(8,128)S(1)} all-to-all(f32[8,80,256]{2,1,0:T(8,128)S(1)} %combine.1), channel_id=1, replica_groups=mesh['mem'=8,'space'=32] {'mem'}, dimensions={0} | all-to-all | bytes 1310720 | tf_op jit(solution)/shard_map/all_to_all | solution.py:386
  54.6 1.6 %blend.1 = f32[4,5,8,16,256]{4,3,2,1,0:T(8,128)} custom-call(s32[1]{0:T(128)} %bitcast.parity_ref, f32[8,80,256]{2,1,0:T(8,128)S(1)} %all_to_all.11.mean, f32[4,5,6,16,256]{4,3,2,1,0:T(8,128)S(1)} %get-tuple-element.23.core, f32[4,3,2,16,256]{4,3,2,1,0:T(8,128)S(1)} %get-tuple-element.24.edge, f32[4,2,2,16,256]{4,3,2,1,0:T(8,128)S(1)} %edges_rest.1.rest), custom_call_target="tpu_custom_call" | custom-call | tf_op jit(solution)/shard_map/blend/pallas_call | solution.py:387
  (2 shorter events, 0.0 us)
Async XLA Ops:
  0.0 1.6 %slice-start = ((f32[4,5,8,16,256]{4,3,2,1,0:T(8,128)}), f32[4,3,8,16,256]{4,3,2,1,0:T(8,128)S(1)}, s32[]{:S(2)}) async-start(f32[4,5,8,16,256]{4,3,2,1,0:T(8,128)} %state.5), calls=%async_computation.2 | async-start | bytes 3145728 | tf_op jit(solution)/shard_map/slice | solution.py:324
  0.0 4.8 %copy-start.1 = (f32[5]{0:T(128)S(1)}, f32[5]{0:T(128)}, u32[]{:S(2)}) copy-start(f32[5]{0:T(128)} %diffusion.5) | copy-start | bytes 64
  0.0 4.9 %copy-start.2 = (s32[16]{0:T(128)S(1)}, s32[16]{0:T(128)}, u32[]{:S(2)}) copy-start(s32[16]{0:T(128)} %radius.1) | copy-start | bytes 196
  0.0 4.9 %copy-start.3 = (s32[1,128]{1,0:T(1,128)S(1)}, s32[1,128]{1,0:T(1,128)}, u32[]{:S(2)}) copy-start(s32[1,128]{1,0:T(1,128)} %cells.1) | copy-start | bytes 1540
  0.0 4.9 %copy-start.4 = (f32[1,128]{1,0:T(1,128)S(1)}, f32[1,128]{1,0:T(1,128)}, u32[]{:S(2)}) copy-start(f32[1,128]{1,0:T(1,128)} %value.1) | copy-start | bytes 1540
  0.0 4.9 %copy-start.5 = (f32[1,128]{1,0:T(1,128)S(1)}, f32[1,128]{1,0:T(1,128)}, u32[]{:S(2)}) copy-start(f32[1,128]{1,0:T(1,128)} %error.1) | copy-start | bytes 1540
  1.3 3.5 %collective-permute-start = (f32[4,5,2,16,256]{4,3,2,1,0:T(8,128)S(1)}, f32[4,5,2,16,256]{4,3,2,1,0:T(8,128)S(1)}, u32[]{:S(2)}, u32[]{:S(2)}) collective-permute-start(f32[4,5,2,16,256]{4,3,2,1,0:T(8,128)S(1)} %constant_dynamic-slice_fusion.1), channel_id=1, source_target_pairs={{0,1},{1,0},{2,3},{3,2},{4,5},{5,4},{6,7},{7,6},{8,9},{9,8},{10,11... | collective-permute-start | bytes 1966088 | tf_op jit(solution)/shard_map/ppermute | solution.py:325
  1.6 12.4 %collective-permute-start.1 = (f32[4,3,2,16,256]{4,3,2,1,0:T(8,128)S(1)}, f32[4,3,2,16,256]{4,3,2,1,0:T(8,128)S(1)}, u32[]{:S(2)}, u32[]{:S(2)}) collective-permute-start(f32[4,3,2,16,256]{4,3,2,1,0:T(8,128)S(1)} %constant_dynamic-slice_fusion), channel_id=1, source_target_pairs={{0,31},{1,2},{2,1},{3,4},{4,3},{5,6},{6,5},{7,8},{8,7},{9,10},{10,... | collective-permute-start | bytes 1179656 | tf_op jit(solution)/shard_map/ppermute | solution.py:326
  4.9 1.7 %copy-start = (f32[4,5,8,16,256]{4,3,2,1,0:T(8,128)S(1)}, f32[4,5,8,16,256]{4,3,2,1,0:T(8,128)}, u32[]{:S(2)}) copy-start(f32[4,5,8,16,256]{4,3,2,1,0:T(8,128)} %state.5) | copy-start | bytes 7864324
  11.0 9.6 %collective-permute-start.4 = (f32[4,2,2,16,256]{4,3,2,1,0:T(8,128)S(1)}, f32[4,2,2,16,256]{4,3,2,1,0:T(8,128)S(1)}, u32[]{:S(2)}, u32[]{:S(2)}) collective-permute-start(f32[4,2,2,16,256]{4,3,2,1,0:T(8,128)S(1)} %get-tuple-element.25), channel_id=1, source_target_pairs={{0,31},{1,2},{2,1},{3,4},{4,3},{5,6},{6,5},{7,8},{8,7},{9,10},{10,... | collective-permute-start | bytes 786440 | tf_op jit(solution)/shard_map/ppermute | solution.py:344
  14.9 7.1 %collective-permute-start.3 = (f32[4,8,256]{2,1,0:T(8,128)S(1)}, f32[4,8,256]{2,1,0:T(8,128)S(1)}, u32[]{:S(2)}, u32[]{:S(2)}) collective-permute-start(f32[4,8,256]{2,1,0:T(8,128)S(1)} %get-tuple-element.22.own), channel_id=1, source_target_pairs={{0,31},{1,2},{2,1},{3,4},{4,3},{5,6},{6,5},{7,8},{8,7},{9,10},{10,... | collective-permute-start | bytes 98312 | tf_op jit(solution)/shard_map/ppermute | solution.py:358
  17.5 4.6 %collective-permute-start.2 = (f32[4,8,256]{2,1,0:T(8,128)S(1)}, f32[4,8,256]{2,1,0:T(8,128)S(1)}, u32[]{:S(2)}, u32[]{:S(2)}) collective-permute-start(f32[4,8,256]{2,1,0:T(8,128)S(1)} %get-tuple-element.22.own), channel_id=1, source_target_pairs={{0,1},{1,0},{2,3},{3,2},{4,5},{5,4},{6,7},{7,6},{8,9},{9,8},{10,11... | collective-permute-start | bytes 98312 | tf_op jit(solution)/shard_map/ppermute | solution.py:357

commit v4 on v3

--- a/solution.py
+++ b/solution.py
@@ -317,6 +317,9 @@
     beside_pairs = [(i, i + 1 - 2 * (i % 2)) for i in range(size)]
     beyond_pairs = [(i, (i - 1 + 2 * (i % 2)) % size) for i in range(size)]
 
+    orders = ((0, 2, 4, 6, 1, 3, 5, 7), (6, 4, 2, 0, 7, 5, 3, 1))
+    groups = [[m * size + t for m in orders[t % 2]] for t in range(size)]
+
     def shape(*dims):
         return jax.ShapeDtypeStruct(dims, f32)
 
@@ -375,7 +378,7 @@
         name="weights",
         compiler_params=room,
     )(parity, level_radius, grid, beside, beyond, core, edge, rest)
-    parts = lax.all_to_all(sends, "mem", 0, 0, tiled=True)
+    parts = lax.all_to_all(sends, ("mem", "space"), 0, 0, tiled=True, axis_index_groups=groups)
     share = pl.pallas_call(
         combine_kernel,
         out_shape=shape(width, 80, lat_cells),
@@ -383,7 +386,7 @@
         name="combine",
         compiler_params=room,
     )(level_radius, parts)
-    mean = lax.all_to_all(share, "mem", 0, 0, tiled=True)
+    mean = lax.all_to_all(share, ("mem", "space"), 0, 0, tiled=True, axis_index_groups=groups)
     return pl.pallas_call(
         blend_kernel,
         out_shape=shape(*state.shape),

time: 57 us -> 55.9 us (0.981)
  blocking collectives: 31.4 us -> 30.7 us
    all_to_all x2, blocking collectives: 31.4 us -> 30.7 us  [the longest x1 16.8 us: local(): lax.all_to_all(sends, ('mem', 'space'), 0, 0, tiled=True, axis_index_grou...]
where the time goes in v4:
time: 55.9 us; the launch traced here: 55.4 us
  blocking collectives  30.7 us (55%)
  starting transfers between devices  9.47 us (17%)
  Pallas kernels  8.71 us (16%)
  local copies, waits for them, and re-layouts  3.24 us (6%)
  waiting for transfers between devices  2.54 us (5%)
  between operations  0.8 us (1%)
    all_to_all x1, blocking collectives, local(): lax.all_to_all(sends, ('mem', 'space'), 0, 0, tiled=True, axis_index_grou...  16.8 us
    all_to_all x1, blocking collectives, local(): lax.all_to_all(share, ('mem', 'space'), 0, 0, tiled=True, axis_index_grou...  13.9 us
    pallas_call x1, Pallas kernels, local(): pl.pallas_call(interior_kernel, out_shape=(shape(members, fields, 6, leve...  4.39 us
    ppermute x1, starting transfers between devices, local(): far_b = lax.ppermute(far_b, 'space', beyond_pairs)  2.99 us
    ppermute x1, starting transfers between devices, local(): beyond = lax.ppermute(grid, 'space', beyond_pairs)  2.55 us
    ppermute x1, starting transfers between devices, local(): far_a = lax.ppermute(far_a, 'space', beyond_pairs)  2.55 us
    ppermute x1, waiting for transfers between devices, local(): far_b = lax.ppermute(far_b, 'space', beyond_pairs)  1.87 us
    unnamed x12, local copies, waits for them, and re-layouts  1.76 us
  transfers between devices with their start and end apart: 5, of which 2 were waited for; matrix products, arithmetic and copies ran while one was open for 0% of the time, Pallas kernels for 11%

profile of v4, /device:TPU:128, one launch (start us, length us, event | category | flops | bytes accessed | tf_op | source)
XLA Modules:
  0.0 55.4 jit_solution(5789738320728479380)
XLA Ops:
  0.0 0.0 slice-start
  0.0 0.0 copy-start.2
  0.0 0.0 copy-start.3
  0.0 0.0 copy-start.4
  0.0 0.0 copy-start.5
  0.0 1.3 %constant_dynamic-slice_fusion.1 = f32[4,5,2,16,256]{4,3,2,1,0:T(8,128)S(1)} fusion(f32[4,5,8,16,256]{4,3,2,1,0:T(8,128)} %state.5, s32[]{:T(128)S(6)} %select_n.6), kind=kLoop, calls=%fused_computation.1 | loop fusion | bytes 1310724 | tf_op jit(solution)/shard_map/dynamic_slice | solution.py:326
  1.3 0.1 collective-permute-start
  1.4 0.2 slice-done
  1.6 2.5 %collective-permute-start.1 = (f32[4,3,2,16,256]{4,3,2,1,0:T(8,128)S(1)}, f32[4,3,2,16,256]{4,3,2,1,0:T(8,128)S(1)}, u32[]{:S(2)}, u32[]{:S(2)}) collective-permute-start(f32[4,3,2,16,256]{4,3,2,1,0:T(8,128)S(1)} %constant_dynamic-slice_fusion), channel_id=1, source_target_pairs={{0,31},{1,2},{2,1},{3,4},{4,3},{5,6},{6,5},{7,8},{8,7},{9,10},{10,... | collective-permute-start | bytes 1179656 | tf_op jit(solution)/shard_map/ppermute | solution.py:329
  4.8 0.0 collective-permute-done.near
  4.8 0.0 copy-done.1
  4.9 0.0 copy-done.2
  4.9 0.0 copy-done.3
  4.9 0.0 copy-done.4
  4.9 0.0 copy-done.5
  4.9 0.0 copy-start
  4.9 1.7 %copy-done = f32[4,5,8,16,256]{4,3,2,1,0:T(8,128)S(1)} copy-done((f32[4,5,8,16,256]{4,3,2,1,0:T(8,128)S(1)}, f32[4,5,8,16,256]{4,3,2,1,0:T(8,128)}, u32[]{:S(2)}) %copy-start) | copy-done | bytes 2621464
  6.6 4.4 %interior.1 = (f32[4,5,6,16,256]{4,3,2,1,0:T(8,128)S(1)}, f32[4,5,16,256]{3,2,1,0:T(8,128)S(1)}, f32[4,5,16,256]{3,2,1,0:T(8,128)S(1)}, f32[4,5,16,256]{3,2,1,0:...) custom-call(s32[1]{0:T(128)} %bitcast.parity_ref, ...), custom_call_target="tpu_custom_call" | custom-call | tf_op jit(solution)/shard_map/interior/pallas_call | solution.py:330
  11.0 3.0 %collective-permute-start.4 = (f32[4,2,2,16,256]{4,3,2,1,0:T(8,128)S(1)}, f32[4,2,2,16,256]{4,3,2,1,0:T(8,128)S(1)}, u32[]{:S(2)}, u32[]{:S(2)}) collective-permute-start(f32[4,2,2,16,256]{4,3,2,1,0:T(8,128)S(1)} %get-tuple-element.25), channel_id=1, source_target_pairs={{0,31},{1,2},{2,1},{3,4},{4,3},{5,6},{6,5},{7,8},{8,7},{9,10},{10,... | collective-permute-start | bytes 786440 | tf_op jit(solution)/shard_map/ppermute | solution.py:347
  14.0 0.0 collective-permute-done.1.far.far_winds_ref
  14.0 0.9 %edges.1 = (f32[4,3,2,16,256]{4,3,2,1,0:T(8,128)S(1)}, f32[4,2,16,256]{3,2,1,0:T(8,128)S(1)}, f32[4,8,256]{2,1,0:T(8,128)S(1)}) custom-call(s32[1]{0:T(128)} %bitcast.parity_ref, f32[4,5,8,16,256]{4,3,2,1,0:T(8,128)S(1)} %copy-done, f32[5]{0:T(128)S(1)} %copy-done.1, f32[4,3,2,16,256]{4,3,2,1,0:T(8,128)S(1)} %collective-permute-done.1.far.far_winds_ref, ...), custom_call_target="tpu_custom_call" | custom-call | tf_op jit(solution)/shard_map/edges/pallas_call | solution.py:348
  14.9 2.5 %collective-permute-start.3 = (f32[4,8,256]{2,1,0:T(8,128)S(1)}, f32[4,8,256]{2,1,0:T(8,128)S(1)}, u32[]{:S(2)}, u32[]{:S(2)}) collective-permute-start(f32[4,8,256]{2,1,0:T(8,128)S(1)} %get-tuple-element.22.own), channel_id=1, source_target_pairs={{0,31},{1,2},{2,1},{3,4},{4,3},{5,6},{6,5},{7,8},{8,7},{9,10},{10,... | collective-permute-start | bytes 98312 | tf_op jit(solution)/shard_map/ppermute | solution.py:361
  17.5 1.3 %collective-permute-start.2 = (f32[4,8,256]{2,1,0:T(8,128)S(1)}, f32[4,8,256]{2,1,0:T(8,128)S(1)}, u32[]{:S(2)}, u32[]{:S(2)}) collective-permute-start(f32[4,8,256]{2,1,0:T(8,128)S(1)} %get-tuple-element.22.own), channel_id=1, source_target_pairs={{0,1},{1,0},{2,3},{3,2},{4,5},{5,4},{6,7},{7,6},{8,9},{9,8},{10,11... | collective-permute-start | bytes 98312 | tf_op jit(solution)/shard_map/ppermute | solution.py:360
  18.8 1.9 %collective-permute-done.4.far = f32[4,2,2,16,256]{4,3,2,1,0:T(8,128)S(1)} collective-permute-done((f32[4,2,2,16,256]{4,3,2,1,0:T(8,128)S(1)}, f32[4,2,2,16,256]{4,3,2,1,0:T(8,128)S(1)}, u32[]{:S(2)}, u32[]{:S(2)}) %collective-permute-start.4) | collective-permute-done | bytes 262176 | tf_op jit(solution)/shard_map/ppermute | solution.py:347
  20.6 0.8 %edges_rest.1.rest = f32[4,2,2,16,256]{4,3,2,1,0:T(8,128)S(1)} custom-call(s32[1]{0:T(128)} %bitcast.parity_ref, f32[4,5,8,16,256]{4,3,2,1,0:T(8,128)S(1)} %copy-done, f32[5]{0:T(128)S(1)} %copy-done.1, f32[4,3,2,16,256]{4,3,2,1,0:T(8,128)S(1)} %collective-permute-done.1.far.far_winds_ref, f32[4,2,2,16,256]{4,3,2,1,0:T(8,128)S(1)} %collective-permute-done.4.far, ...), custom_call_target="tpu_custom_call" | custom-call | tf_op jit(solution)/shard_map/edges_rest/pallas_call | solution.py:362
  21.4 0.7 %collective-permute-done.3.beyond = f32[4,8,256]{2,1,0:T(8,128)S(1)} collective-permute-done((f32[4,8,256]{2,1,0:T(8,128)S(1)}, f32[4,8,256]{2,1,0:T(8,128)S(1)}, u32[]{:S(2)}, u32[]{:S(2)}) %collective-permute-start.3) | collective-permute-done | bytes 32800 | tf_op jit(solution)/shard_map/ppermute | solution.py:361
  22.1 0.0 collective-permute-done.2.beside
  22.1 1.0 %weights.1 = f32[8,88,256]{2,1,0:T(8,128)S(1)} custom-call(s32[1]{0:T(128)} %bitcast.parity_ref, s32[16,256]{1,0:T(8,128)S(1)} %get-tuple-element.16.level_radius, f32[4,8,256]{2,1,0:T(8,128)S(1)} %get-tuple-element.22.own, f32[4,8,256]{2,1,0:T(8,128)S(1)} %collective-permute-done.2.beside, f32[4,8,256]{2,1,0:T(8,128)S(1)} %collective-permute-done.3.beyond, ...), custom_call_target="tpu_custom_call" | custom-call | tf_op jit(solution)/shard_map/weights/pallas_call | solution.py:369
  23.0 16.8 %all_to_all.10.parts = f32[8,88,256]{2,1,0:T(8,128)S(1)} all-to-all(f32[8,88,256]{2,1,0:T(8,128)S(1)} %weights.1), channel_id=1, replica_groups={{0,64,128,192,32,96,160,224},{193,129,65,1,225,161,97,33},{2,66,130,194..., dimensions={0} | all-to-all | bytes 1441792 | tf_op jit(solution)/shard_map/all_to_all | solution.py:381
  39.8 0.1 combine.1
  39.9 13.9 %all_to_all.11.mean = f32[8,80,256]{2,1,0:T(8,128)S(1)} all-to-all(f32[8,80,256]{2,1,0:T(8,128)S(1)} %combine.1), channel_id=1, replica_groups={{0,64,128,192,32,96,160,224},{193,129,65,1,225,161,97,33},{2,66,130,194..., dimensions={0} | all-to-all | bytes 1310720 | tf_op jit(solution)/shard_map/all_to_all | solution.py:389
  53.8 1.6 %blend.1 = f32[4,5,8,16,256]{4,3,2,1,0:T(8,128)} custom-call(s32[1]{0:T(128)} %bitcast.parity_ref, f32[8,80,256]{2,1,0:T(8,128)S(1)} %all_to_all.11.mean, f32[4,5,6,16,256]{4,3,2,1,0:T(8,128)S(1)} %get-tuple-element.23.core, f32[4,3,2,16,256]{4,3,2,1,0:T(8,128)S(1)} %get-tuple-element.24.edge, f32[4,2,2,16,256]{4,3,2,1,0:T(8,128)S(1)} %edges_rest.1.rest), custom_call_target="tpu_custom_call" | custom-call | tf_op jit(solution)/shard_map/blend/pallas_call | solution.py:390
  (2 shorter events, 0.0 us)
Async XLA Ops:
  0.0 1.6 %slice-start = ((f32[4,5,8,16,256]{4,3,2,1,0:T(8,128)}), f32[4,3,8,16,256]{4,3,2,1,0:T(8,128)S(1)}, s32[]{:S(2)}) async-start(f32[4,5,8,16,256]{4,3,2,1,0:T(8,128)} %state.5), calls=%async_computation.2 | async-start | bytes 3145728 | tf_op jit(solution)/shard_map/slice | solution.py:327
  0.0 4.8 %copy-start.1 = (f32[5]{0:T(128)S(1)}, f32[5]{0:T(128)}, u32[]{:S(2)}) copy-start(f32[5]{0:T(128)} %diffusion.5) | copy-start | bytes 64
  0.0 4.9 %copy-start.2 = (s32[16]{0:T(128)S(1)}, s32[16]{0:T(128)}, u32[]{:S(2)}) copy-start(s32[16]{0:T(128)} %radius.1) | copy-start | bytes 196
  0.0 4.9 %copy-start.3 = (s32[1,128]{1,0:T(1,128)S(1)}, s32[1,128]{1,0:T(1,128)}, u32[]{:S(2)}) copy-start(s32[1,128]{1,0:T(1,128)} %cells.1) | copy-start | bytes 1540
  0.0 4.9 %copy-start.4 = (f32[1,128]{1,0:T(1,128)S(1)}, f32[1,128]{1,0:T(1,128)}, u32[]{:S(2)}) copy-start(f32[1,128]{1,0:T(1,128)} %value.1) | copy-start | bytes 1540
  0.0 4.9 %copy-start.5 = (f32[1,128]{1,0:T(1,128)S(1)}, f32[1,128]{1,0:T(1,128)}, u32[]{:S(2)}) copy-start(f32[1,128]{1,0:T(1,128)} %error.1) | copy-start | bytes 1540
  1.3 3.5 %collective-permute-start = (f32[4,5,2,16,256]{4,3,2,1,0:T(8,128)S(1)}, f32[4,5,2,16,256]{4,3,2,1,0:T(8,128)S(1)}, u32[]{:S(2)}, u32[]{:S(2)}) collective-permute-start(f32[4,5,2,16,256]{4,3,2,1,0:T(8,128)S(1)} %constant_dynamic-slice_fusion.1), channel_id=1, source_target_pairs={{0,1},{1,0},{2,3},{3,2},{4,5},{5,4},{6,7},{7,6},{8,9},{9,8},{10,11... | collective-permute-start | bytes 1966088 | tf_op jit(solution)/shard_map/ppermute | solution.py:328
  1.6 12.4 %collective-permute-start.1 = (f32[4,3,2,16,256]{4,3,2,1,0:T(8,128)S(1)}, f32[4,3,2,16,256]{4,3,2,1,0:T(8,128)S(1)}, u32[]{:S(2)}, u32[]{:S(2)}) collective-permute-start(f32[4,3,2,16,256]{4,3,2,1,0:T(8,128)S(1)} %constant_dynamic-slice_fusion), channel_id=1, source_target_pairs={{0,31},{1,2},{2,1},{3,4},{4,3},{5,6},{6,5},{7,8},{8,7},{9,10},{10,... | collective-permute-start | bytes 1179656 | tf_op jit(solution)/shard_map/ppermute | solution.py:329
  4.9 1.7 %copy-start = (f32[4,5,8,16,256]{4,3,2,1,0:T(8,128)S(1)}, f32[4,5,8,16,256]{4,3,2,1,0:T(8,128)}, u32[]{:S(2)}) copy-start(f32[4,5,8,16,256]{4,3,2,1,0:T(8,128)} %state.5) | copy-start | bytes 7864324
  11.0 9.6 %collective-permute-start.4 = (f32[4,2,2,16,256]{4,3,2,1,0:T(8,128)S(1)}, f32[4,2,2,16,256]{4,3,2,1,0:T(8,128)S(1)}, u32[]{:S(2)}, u32[]{:S(2)}) collective-permute-start(f32[4,2,2,16,256]{4,3,2,1,0:T(8,128)S(1)} %get-tuple-element.25), channel_id=1, source_target_pairs={{0,31},{1,2},{2,1},{3,4},{4,3},{5,6},{6,5},{7,8},{8,7},{9,10},{10,... | collective-permute-start | bytes 786440 | tf_op jit(solution)/shard_map/ppermute | solution.py:347
  14.9 7.1 %collective-permute-start.3 = (f32[4,8,256]{2,1,0:T(8,128)S(1)}, f32[4,8,256]{2,1,0:T(8,128)S(1)}, u32[]{:S(2)}, u32[]{:S(2)}) collective-permute-start(f32[4,8,256]{2,1,0:T(8,128)S(1)} %get-tuple-element.22.own), channel_id=1, source_target_pairs={{0,31},{1,2},{2,1},{3,4},{4,3},{5,6},{6,5},{7,8},{8,7},{9,10},{10,... | collective-permute-start | bytes 98312 | tf_op jit(solution)/shard_map/ppermute | solution.py:361
  17.5 4.6 %collective-permute-start.2 = (f32[4,8,256]{2,1,0:T(8,128)S(1)}, f32[4,8,256]{2,1,0:T(8,128)S(1)}, u32[]{:S(2)}, u32[]{:S(2)}) collective-permute-start(f32[4,8,256]{2,1,0:T(8,128)S(1)} %get-tuple-element.22.own), channel_id=1, source_target_pairs={{0,1},{1,0},{2,3},{3,2},{4,5},{5,4},{6,7},{7,6},{8,9},{9,8},{10,11... | collective-permute-start | bytes 98312 | tf_op jit(solution)/shard_map/ppermute | solution.py:360

commit v5 on v4

--- a/solution.py
+++ b/solution.py
@@ -44,12 +44,12 @@
 
 
 def interior_kernel(
-    parity_ref, state, near, diffusion, radius, cells, count, value, error,
-    core, once_one, pre_zero, pre_one, column, grids, level_radius, far, once,
+    state, near, diffusion, radius, cells, count, value, error,
+    core, once_one, pre_zero, pre_one, column, grids, level_radius, far, rates, once,
 ):
     sites = cells.shape[1]
     lat_cells = state.shape[4]
-    parity = parity_ref[0]
+    parity = lax.rem(lax.axis_index("space"), 2)
     half = 0.5 * time_step
     signed = half * (1 - 2 * parity).astype(f32)
     far_start = 6 * parity
@@ -109,6 +109,9 @@
     grids[0] = total
     grids[1] = mean
     grids[2] = second - first * mean
+    for f in range(5):
+        rates[f : f + 1] = jnp.full((1, lat_cells), diffusion[f] * time_step, f32)
+    rates[5:8] = jnp.zeros((3, lat_cells), f32)
     levels = level_radius.shape[0]
     level = lax.broadcasted_iota(jnp.int32, (levels, lat_cells), 0)
     chosen = jnp.full((levels, lat_cells), radius[0], jnp.int32)
@@ -143,9 +146,9 @@
 
 
 def far_kernel(
-    parity_ref, state, diffusion, far, once_one, pre_zero, pre_one, column, grids, edge, winds_out, grid, full
+    state, rates, far, once_one, pre_zero, pre_one, column, grids, edge, winds_out, grid, full
 ):
-    parity = parity_ref[0]
+    parity = lax.rem(lax.axis_index("space"), 2)
     half = 0.5 * time_step
     signed = half * (1 - 2 * parity).astype(f32)
 
@@ -154,7 +157,7 @@
         pairs = [
             far_rows(
                 far[m, f, parity], far[m, f, 1 - parity], state[m, f, natural(0, parity)],
-                once_one[m, f], pre_zero[m, f], pre_one[m, f], winds, diffusion[f] * time_step,
+                once_one[m, f], pre_zero[m, f], pre_one[m, f], winds, rates[f : f + 1],
             )
             for f in range(3)
         ]
@@ -174,15 +177,15 @@
     lax.fori_loop(0, state.shape[0], member, 0, unroll=True)
 
 
-def far_rest_kernel(parity_ref, state, diffusion, far_winds_ref, far, once_one, pre_zero, pre_one, winds_in, edge):
-    parity = parity_ref[0]
+def far_rest_kernel(state, rates, far_winds_ref, far, once_one, pre_zero, pre_one, winds_in, edge):
+    parity = lax.rem(lax.axis_index("space"), 2)
 
     def member(m, carry):
         winds = far_winds(m, parity, state, far_winds_ref, once_one)
         for f in (3, 4):
             _, again = far_rows(
                 far[m, f - 3, parity], far[m, f - 3, 1 - parity], state[m, f, natural(0, parity)],
-                once_one[m, f], pre_zero[m, f], pre_one[m, f], winds, diffusion[f] * time_step,
+                once_one[m, f], pre_zero[m, f], pre_one[m, f], winds, rates[f : f + 1],
             )
             for k, row in enumerate(again(winds_in[m, 0], winds_in[m, 1])):
                 edge[m, f - 3, k] = row
@@ -204,10 +207,10 @@
     return edge[m, f, k] if f < 3 else rest[m, f - 3, k]
 
 
-def weights_kernel(parity_ref, level_radius, own, beside, beyond, core, edge, rest, sends, near, shifted, expo):
+def weights_kernel(level_radius, own, beside, beyond, core, edge, rest, sends, near, shifted, expo):
     members, width, lat_cells = own.shape
     half = lat_cells // 2
-    parity = parity_ref[0]
+    parity = lax.rem(lax.axis_index("space"), 2)
 
     def convolve(m, carry):
         near[m, pl.ds(16 * parity, 8)] = beyond[m]
@@ -292,9 +295,9 @@
             result[d, 16 * f : 16 * f + 16] = sums[f]
 
 
-def blend_kernel(parity_ref, mean, core, edge, rest, out, done, sems):
+def blend_kernel(mean, core, edge, rest, out, done, sems):
     members = core.shape[0]
-    parity = parity_ref[0]
+    parity = lax.rem(lax.axis_index("space"), 2)
     copies = []
     for m in range(members):
         for part in range(2):
@@ -327,7 +330,7 @@
     far_a = lax.dynamic_slice_in_dim(state[:, :3], 6 * parity[0], 2, axis=2)
     near = lax.ppermute(near, "space", beside_pairs)
     far_a = lax.ppermute(far_a, "space", beyond_pairs)
-    core, once_one, pre_zero, pre_one, column, grids, level_radius, far_b = pl.pallas_call(
+    core, once_one, pre_zero, pre_one, column, grids, level_radius, far_b, rates = pl.pallas_call(
         interior_kernel,
         out_shape=(
             shape(members, fields, 6, levels, lat_cells),
@@ -338,12 +341,13 @@
             shape(3, width, lat_cells),
             jax.ShapeDtypeStruct((levels, lat_cells), jnp.int32),
             shape(members, 2, 2, levels, lat_cells),
+            shape(8, lat_cells),
         ),
-        in_specs=[smem, vmem, vmem, smem, smem, vmem, smem, vmem, vmem],
+        in_specs=[vmem, vmem, smem, smem, vmem, smem, vmem, vmem],
         scratch_shapes=[pltpu.VMEM((fields, 8, levels, lat_cells), f32)],
         name="interior",
         compiler_params=room,
-    )(parity, state, near, diffusion, radius, obs_cells, obs_count, obs_value, obs_error)
+    )(state, near, diffusion, radius, obs_cells, obs_count, obs_value, obs_error)
     far_b = lax.ppermute(far_b, "space", beyond_pairs)
     edge, winds, grid = pl.pallas_call(
         far_kernel,
@@ -352,24 +356,24 @@
             shape(members, 2, levels, lat_cells),
             shape(members, width, lat_cells),
         ),
-        in_specs=[smem, vmem, smem] + [vmem] * 6,
+        in_specs=[vmem] * 8,
         scratch_shapes=[pltpu.VMEM((members, width, lat_cells), f32)],
         name="edges",
         compiler_params=room,
-    )(parity, state, diffusion, far_a, once_one, pre_zero, pre_one, column, grids)
+    )(state, rates, far_a, once_one, pre_zero, pre_one, column, grids)
     beside = lax.ppermute(grid, "space", beside_pairs)
     beyond = lax.ppermute(grid, "space", beyond_pairs)
     rest = pl.pallas_call(
         far_rest_kernel,
         out_shape=shape(members, 2, 2, levels, lat_cells),
-        in_specs=[smem, vmem, smem] + [vmem] * 6,
+        in_specs=[vmem] * 8,
         name="edges_rest",
         compiler_params=room,
-    )(parity, state, diffusion, far_a, far_b, once_one, pre_zero, pre_one, winds)
+    )(state, rates, far_a, far_b, once_one, pre_zero, pre_one, winds)
     sends = pl.pallas_call(
         weights_kernel,
         out_shape=shape(width, 88, lat_cells),
-        in_specs=[smem] + [vmem] * 7,
+        in_specs=[vmem] * 7,
         scratch_shapes=[
             pltpu.VMEM((members, 24, lat_cells), f32),
             pltpu.VMEM((members, reach + 1, 2, 24, lat_cells // 2), f32),
@@ -377,7 +381,7 @@
         ],
         name="weights",
         compiler_params=room,
-    )(parity, level_radius, grid, beside, beyond, core, edge, rest)
+    )(level_radius, grid, beside, beyond, core, edge, rest)
     parts = lax.all_to_all(sends, ("mem", "space"), 0, 0, tiled=True, axis_index_groups=groups)
     share = pl.pallas_call(
         combine_kernel,
@@ -390,12 +394,12 @@
     return pl.pallas_call(
         blend_kernel,
         out_shape=shape(*state.shape),
-        in_specs=[smem] + [vmem] * 4,
+        in_specs=[vmem] * 4,
         out_specs=anywhere,
         scratch_shapes=[pltpu.VMEM(state.shape, f32), pltpu.SemaphoreType.DMA((members, 2))],
         name="blend",
         compiler_params=room,
-    )(parity, mean, core, edge, rest)
+    )(mean, core, edge, rest)
 
 
 def solution(mesh):

time: 55.9 us -> 55.3 us (0.989)
  Pallas kernels: 8.71 us -> 7.53 us
  transfers between devices with their start and end apart: 5 -> 5, of which waited for: 2 -> 2; matrix products, arithmetic and copies ran while one was open for 0% -> 0% of each run, Pallas kernels for 11% -> 9%
where the time goes in v5:
time: 55.3 us; the launch traced here: 54.8 us
  blocking collectives  30.8 us (56%)
  starting transfers between devices  9.64 us (17%)
  Pallas kernels  7.53 us (14%)
  local copies, waits for them, and re-layouts  3.24 us (6%)
  waiting for transfers between devices  2.81 us (5%)
  between operations  0.8 us (1%)
    all_to_all x1, blocking collectives, local(): lax.all_to_all(sends, ('mem', 'space'), 0, 0, tiled=True, axis_index_grou...  16.9 us
    all_to_all x1, blocking collectives, local(): lax.all_to_all(share, ('mem', 'space'), 0, 0, tiled=True, axis_index_grou...  13.8 us
    pallas_call x1, Pallas kernels, local(): pl.pallas_call(interior_kernel, out_shape=(shape(members, fields, 6, leve...  4.22 us
    ppermute x1, starting transfers between devices, local(): far_b = lax.ppermute(far_b, 'space', beyond_pairs)  2.99 us
    ppermute x1, starting transfers between devices, local(): far_a = lax.ppermute(far_a, 'space', beyond_pairs)  2.55 us
    ppermute x1, starting transfers between devices, local(): beyond = lax.ppermute(grid, 'space', beyond_pairs)  2.55 us
    ppermute x1, waiting for transfers between devices, local(): far_b = lax.ppermute(far_b, 'space', beyond_pairs)  2.24 us
    unnamed x12, local copies, waits for them, and re-layouts  1.76 us
  transfers between devices with their start and end apart: 5, of which 2 were waited for; matrix products, arithmetic and copies ran while one was open for 0% of the time, Pallas kernels for 9%

profile of v5, /device:TPU:128, one launch (start us, length us, event | category | flops | bytes accessed | tf_op | source)
XLA Modules:
  0.0 54.8 jit_solution(3119387508366793865)
XLA Ops:
  0.0 0.0 slice-start
  0.0 0.0 copy-start.1
  0.0 0.0 copy-start.3
  0.0 0.0 copy-start.4
  0.0 0.0 copy-start.5
  0.0 1.3 %constant_dynamic-slice_fusion.1 = f32[4,5,2,16,256]{4,3,2,1,0:T(8,128)S(1)} fusion(f32[4,5,8,16,256]{4,3,2,1,0:T(8,128)} %state.5, s32[]{:T(128)S(6)} %select_n.6), kind=kLoop, calls=%fused_computation.1 | loop fusion | bytes 1310724 | tf_op jit(solution)/shard_map/dynamic_slice | solution.py:329
  1.3 0.1 collective-permute-start
  1.4 0.2 slice-done
  1.6 2.5 %collective-permute-start.1 = (f32[4,3,2,16,256]{4,3,2,1,0:T(8,128)S(1)}, f32[4,3,2,16,256]{4,3,2,1,0:T(8,128)S(1)}, u32[]{:S(2)}, u32[]{:S(2)}) collective-permute-start(f32[4,3,2,16,256]{4,3,2,1,0:T(8,128)S(1)} %constant_dynamic-slice_fusion), channel_id=1, source_target_pairs={{0,31},{1,2},{2,1},{3,4},{4,3},{5,6},{6,5},{7,8},{8,7},{9,10},{10,... | collective-permute-start | bytes 1179656 | tf_op jit(solution)/shard_map/ppermute | solution.py:332
  4.8 0.0 collective-permute-done.near
  4.8 0.0 copy-done.1
  4.9 0.0 copy-done.2
  4.9 0.0 copy-done.3
  4.9 0.0 copy-done.4
  4.9 0.0 copy-done.5
  4.9 0.0 copy-start
  4.9 1.7 %copy-done = f32[4,5,8,16,256]{4,3,2,1,0:T(8,128)S(1)} copy-done((f32[4,5,8,16,256]{4,3,2,1,0:T(8,128)S(1)}, f32[4,5,8,16,256]{4,3,2,1,0:T(8,128)}, u32[]{:S(2)}) %copy-start) | copy-done | bytes 2621464
  6.6 4.2 %interior.1 = (f32[4,5,6,16,256]{4,3,2,1,0:T(8,128)S(1)}, f32[4,5,16,256]{3,2,1,0:T(8,128)S(1)}, f32[4,5,16,256]{3,2,1,0:T(8,128)S(1)}, f32[4,5,16,256]{3,2,1,0:...) custom-call(f32[4,5,8,16,256]{4,3,2,1,0:T(8,128)S(1)} %copy-done, ...), custom_call_target="tpu_custom_call" | custom-call | tf_op jit(solution)/shard_map/interior/pallas_call | solution.py:333
  10.9 3.0 %collective-permute-start.4 = (f32[4,2,2,16,256]{4,3,2,1,0:T(8,128)S(1)}, f32[4,2,2,16,256]{4,3,2,1,0:T(8,128)S(1)}, u32[]{:S(2)}, u32[]{:S(2)}) collective-permute-start(f32[4,2,2,16,256]{4,3,2,1,0:T(8,128)S(1)} %get-tuple-element.27), channel_id=1, source_target_pairs={{0,31},{1,2},{2,1},{3,4},{4,3},{5,6},{6,5},{7,8},{8,7},{9,10},{10,... | collective-permute-start | bytes 786440 | tf_op jit(solution)/shard_map/ppermute | solution.py:351
  13.9 0.0 collective-permute-done.1.far.far_winds_ref
  13.9 0.3 edges.1
  14.2 2.5 %collective-permute-start.3 = (f32[4,8,256]{2,1,0:T(8,128)S(1)}, f32[4,8,256]{2,1,0:T(8,128)S(1)}, u32[]{:S(2)}, u32[]{:S(2)}) collective-permute-start(f32[4,8,256]{2,1,0:T(8,128)S(1)} %get-tuple-element.24.own), channel_id=1, source_target_pairs={{0,31},{1,2},{2,1},{3,4},{4,3},{5,6},{6,5},{7,8},{8,7},{9,10},{10,... | collective-permute-start | bytes 98312 | tf_op jit(solution)/shard_map/ppermute | solution.py:365
  16.8 1.5 %collective-permute-start.2 = (f32[4,8,256]{2,1,0:T(8,128)S(1)}, f32[4,8,256]{2,1,0:T(8,128)S(1)}, u32[]{:S(2)}, u32[]{:S(2)}) collective-permute-start(f32[4,8,256]{2,1,0:T(8,128)S(1)} %get-tuple-element.24.own), channel_id=1, source_target_pairs={{0,1},{1,0},{2,3},{3,2},{4,5},{5,4},{6,7},{7,6},{8,9},{9,8},{10,11... | collective-permute-start | bytes 98312 | tf_op jit(solution)/shard_map/ppermute | solution.py:364
  18.2 2.2 %collective-permute-done.4.far = f32[4,2,2,16,256]{4,3,2,1,0:T(8,128)S(1)} collective-permute-done((f32[4,2,2,16,256]{4,3,2,1,0:T(8,128)S(1)}, f32[4,2,2,16,256]{4,3,2,1,0:T(8,128)S(1)}, u32[]{:S(2)}, u32[]{:S(2)}) %collective-permute-start.4) | collective-permute-done | bytes 262176 | tf_op jit(solution)/shard_map/ppermute | solution.py:351
  20.5 0.2 edges_rest.1.rest
  20.7 0.6 %collective-permute-done.3.beyond = f32[4,8,256]{2,1,0:T(8,128)S(1)} collective-permute-done((f32[4,8,256]{2,1,0:T(8,128)S(1)}, f32[4,8,256]{2,1,0:T(8,128)S(1)}, u32[]{:S(2)}, u32[]{:S(2)}) %collective-permute-start.3) | collective-permute-done | bytes 32800 | tf_op jit(solution)/shard_map/ppermute | solution.py:365
  21.3 0.0 collective-permute-done.2.beside
  21.3 1.0 %weights.1 = f32[8,88,256]{2,1,0:T(8,128)S(1)} custom-call(s32[16,256]{1,0:T(8,128)S(1)} %get-tuple-element.17.level_radius, f32[4,8,256]{2,1,0:T(8,128)S(1)} %get-tuple-element.24.own, f32[4,8,256]{2,1,0:T(8,128)S(1)} %collective-permute-done.2.beside, f32[4,8,256]{2,1,0:T(8,128)S(1)} %collective-permute-done.3.beyond, ...), custom_call_target="tpu_custom_call" | custom-call | tf_op jit(solution)/shard_map/weights/pallas_call | solution.py:373
  22.3 16.9 %all_to_all.10.parts = f32[8,88,256]{2,1,0:T(8,128)S(1)} all-to-all(f32[8,88,256]{2,1,0:T(8,128)S(1)} %weights.1), channel_id=1, replica_groups={{0,64,128,192,32,96,160,224},{193,129,65,1,225,161,97,33},{2,66,130,194..., dimensions={0} | all-to-all | bytes 1441792 | tf_op jit(solution)/shard_map/all_to_all | solution.py:385
  39.2 0.1 combine.1
  39.4 13.8 %all_to_all.11.mean = f32[8,80,256]{2,1,0:T(8,128)S(1)} all-to-all(f32[8,80,256]{2,1,0:T(8,128)S(1)} %combine.1), channel_id=1, replica_groups={{0,64,128,192,32,96,160,224},{193,129,65,1,225,161,97,33},{2,66,130,194..., dimensions={0} | all-to-all | bytes 1310720 | tf_op jit(solution)/shard_map/all_to_all | solution.py:393
  53.2 1.6 %blend.1 = f32[4,5,8,16,256]{4,3,2,1,0:T(8,128)} custom-call(f32[8,80,256]{2,1,0:T(8,128)S(1)} %all_to_all.11.mean, f32[4,5,6,16,256]{4,3,2,1,0:T(8,128)S(1)} %get-tuple-element.25.core, f32[4,3,2,16,256]{4,3,2,1,0:T(8,128)S(1)} %get-tuple-element.26.edge, f32[4,2,2,16,256]{4,3,2,1,0:T(8,128)S(1)} %edges_rest.1.rest), custom_call_target="tpu_custom_call" | custom-call | tf_op jit(solution)/shard_map/blend/pallas_call | solution.py:394
  (2 shorter events, 0.0 us)
Async XLA Ops:
  0.0 1.6 %slice-start = ((f32[4,5,8,16,256]{4,3,2,1,0:T(8,128)}), f32[4,3,8,16,256]{4,3,2,1,0:T(8,128)S(1)}, s32[]{:S(2)}) async-start(f32[4,5,8,16,256]{4,3,2,1,0:T(8,128)} %state.5), calls=%async_computation.2 | async-start | bytes 3145728 | tf_op jit(solution)/shard_map/slice | solution.py:330
  0.0 4.8 %copy-start.1 = (f32[5]{0:T(128)S(1)}, f32[5]{0:T(128)}, u32[]{:S(2)}) copy-start(f32[5]{0:T(128)} %diffusion.1) | copy-start | bytes 64
  0.0 4.9 %copy-start.2 = (s32[16]{0:T(128)S(1)}, s32[16]{0:T(128)}, u32[]{:S(2)}) copy-start(s32[16]{0:T(128)} %radius.1) | copy-start | bytes 196
  0.0 4.9 %copy-start.3 = (s32[1,128]{1,0:T(1,128)S(1)}, s32[1,128]{1,0:T(1,128)}, u32[]{:S(2)}) copy-start(s32[1,128]{1,0:T(1,128)} %cells.1) | copy-start | bytes 1540
  0.0 4.9 %copy-start.4 = (f32[1,128]{1,0:T(1,128)S(1)}, f32[1,128]{1,0:T(1,128)}, u32[]{:S(2)}) copy-start(f32[1,128]{1,0:T(1,128)} %value.1) | copy-start | bytes 1540
  0.0 4.9 %copy-start.5 = (f32[1,128]{1,0:T(1,128)S(1)}, f32[1,128]{1,0:T(1,128)}, u32[]{:S(2)}) copy-start(f32[1,128]{1,0:T(1,128)} %error.1) | copy-start | bytes 1540
  1.3 3.5 %collective-permute-start = (f32[4,5,2,16,256]{4,3,2,1,0:T(8,128)S(1)}, f32[4,5,2,16,256]{4,3,2,1,0:T(8,128)S(1)}, u32[]{:S(2)}, u32[]{:S(2)}) collective-permute-start(f32[4,5,2,16,256]{4,3,2,1,0:T(8,128)S(1)} %constant_dynamic-slice_fusion.1), channel_id=1, source_target_pairs={{0,1},{1,0},{2,3},{3,2},{4,5},{5,4},{6,7},{7,6},{8,9},{9,8},{10,11... | collective-permute-start | bytes 1966088 | tf_op jit(solution)/shard_map/ppermute | solution.py:331
  1.6 12.2 %collective-permute-start.1 = (f32[4,3,2,16,256]{4,3,2,1,0:T(8,128)S(1)}, f32[4,3,2,16,256]{4,3,2,1,0:T(8,128)S(1)}, u32[]{:S(2)}, u32[]{:S(2)}) collective-permute-start(f32[4,3,2,16,256]{4,3,2,1,0:T(8,128)S(1)} %constant_dynamic-slice_fusion), channel_id=1, source_target_pairs={{0,31},{1,2},{2,1},{3,4},{4,3},{5,6},{6,5},{7,8},{8,7},{9,10},{10,... | collective-permute-start | bytes 1179656 | tf_op jit(solution)/shard_map/ppermute | solution.py:332
  4.9 1.7 %copy-start = (f32[4,5,8,16,256]{4,3,2,1,0:T(8,128)S(1)}, f32[4,5,8,16,256]{4,3,2,1,0:T(8,128)}, u32[]{:S(2)}) copy-start(f32[4,5,8,16,256]{4,3,2,1,0:T(8,128)} %state.5) | copy-start | bytes 7864324
  10.9 9.6 %collective-permute-start.4 = (f32[4,2,2,16,256]{4,3,2,1,0:T(8,128)S(1)}, f32[4,2,2,16,256]{4,3,2,1,0:T(8,128)S(1)}, u32[]{:S(2)}, u32[]{:S(2)}) collective-permute-start(f32[4,2,2,16,256]{4,3,2,1,0:T(8,128)S(1)} %get-tuple-element.27), channel_id=1, source_target_pairs={{0,31},{1,2},{2,1},{3,4},{4,3},{5,6},{6,5},{7,8},{8,7},{9,10},{10,... | collective-permute-start | bytes 786440 | tf_op jit(solution)/shard_map/ppermute | solution.py:351
  14.2 7.0 %collective-permute-start.3 = (f32[4,8,256]{2,1,0:T(8,128)S(1)}, f32[4,8,256]{2,1,0:T(8,128)S(1)}, u32[]{:S(2)}, u32[]{:S(2)}) collective-permute-start(f32[4,8,256]{2,1,0:T(8,128)S(1)} %get-tuple-element.24.own), channel_id=1, source_target_pairs={{0,31},{1,2},{2,1},{3,4},{4,3},{5,6},{6,5},{7,8},{8,7},{9,10},{10,... | collective-permute-start | bytes 98312 | tf_op jit(solution)/shard_map/ppermute | solution.py:365
  16.8 4.5 %collective-permute-start.2 = (f32[4,8,256]{2,1,0:T(8,128)S(1)}, f32[4,8,256]{2,1,0:T(8,128)S(1)}, u32[]{:S(2)}, u32[]{:S(2)}) collective-permute-start(f32[4,8,256]{2,1,0:T(8,128)S(1)} %get-tuple-element.24.own), channel_id=1, source_target_pairs={{0,1},{1,0},{2,3},{3,2},{4,5},{5,4},{6,7},{7,6},{8,9},{9,8},{10,11... | collective-permute-start | bytes 98312 | tf_op jit(solution)/shard_map/ppermute | solution.py:364

commit v6 on v5

--- a/solution.py
+++ b/solution.py
@@ -88,7 +88,7 @@
                 far[m, f - 3, k] = state[m, f, far_start + k]
         return carry
 
-    lax.fori_loop(0, state.shape[0], member, 0)
+    lax.fori_loop(0, state.shape[0], member, 0, unroll=True)
 
     cell = cells[...]
     site_x = cell // lat_cells

time: 55.3 us -> 55.1 us (level)
  transfers between devices with their start and end apart: 5 -> 5, of which waited for: 2 -> 2; matrix products, arithmetic and copies ran while one was open for 0% -> 0% of each run, Pallas kernels for 9% -> 8%
where the time goes in v6:
time: 55.1 us; the launch traced here: 54.3 us
  blocking collectives  30.8 us (56%)
  starting transfers between devices  10.1 us (18%)
  Pallas kernels  7.05 us (13%)
  local copies, waits for them, and re-layouts  3.24 us (6%)
  waiting for transfers between devices  2.34 us (4%)
  between operations  0.79 us (1%)
    all_to_all x1, blocking collectives, local(): lax.all_to_all(sends, ('mem', 'space'), 0, 0, tiled=True, axis_index_grou...  16.9 us
    all_to_all x1, blocking collectives, local(): lax.all_to_all(share, ('mem', 'space'), 0, 0, tiled=True, axis_index_grou...  13.8 us
    pallas_call x1, Pallas kernels, local(): pl.pallas_call(interior_kernel, out_shape=(shape(members, fields, 6, leve...  3.75 us
    ppermute x1, starting transfers between devices, local(): far_b = lax.ppermute(far_b, 'space', beyond_pairs)  2.99 us
    ppermute x1, starting transfers between devices, local(): beyond = lax.ppermute(grid, 'space', beyond_pairs)  2.55 us
    ppermute x1, starting transfers between devices, local(): far_a = lax.ppermute(far_a, 'space', beyond_pairs)  2.55 us
    ppermute x1, starting transfers between devices, local(): beside = lax.ppermute(grid, 'space', beside_pairs)  1.94 us
    ppermute x1, waiting for transfers between devices, local(): far_b = lax.ppermute(far_b, 'space', beyond_pairs)  1.77 us
  transfers between devices with their start and end apart: 5, of which 2 were waited for; matrix products, arithmetic and copies ran while one was open for 0% of the time, Pallas kernels for 8%

profile of v6, /device:TPU:128, one launch (start us, length us, event | category | flops | bytes accessed | tf_op | source)
XLA Modules:
  0.0 54.3 jit_solution(7262829431433947221)
XLA Ops:
  0.0 0.0 slice-start
  0.0 0.0 copy-start.1
  0.0 0.0 copy-start.3
  0.0 0.0 copy-start.4
  0.0 0.0 copy-start.5
  0.0 1.3 %constant_dynamic-slice_fusion.1 = f32[4,5,2,16,256]{4,3,2,1,0:T(8,128)S(1)} fusion(f32[4,5,8,16,256]{4,3,2,1,0:T(8,128)} %state.5, s32[]{:T(128)S(6)} %select_n.6), kind=kLoop, calls=%fused_computation.1 | loop fusion | bytes 1310724 | tf_op jit(solution)/shard_map/dynamic_slice | solution.py:329
  1.3 0.1 collective-permute-start
  1.4 0.2 slice-done
  1.6 2.5 %collective-permute-start.1 = (f32[4,3,2,16,256]{4,3,2,1,0:T(8,128)S(1)}, f32[4,3,2,16,256]{4,3,2,1,0:T(8,128)S(1)}, u32[]{:S(2)}, u32[]{:S(2)}) collective-permute-start(f32[4,3,2,16,256]{4,3,2,1,0:T(8,128)S(1)} %constant_dynamic-slice_fusion), channel_id=1, source_target_pairs={{0,31},{1,2},{2,1},{3,4},{4,3},{5,6},{6,5},{7,8},{8,7},{9,10},{10,... | collective-permute-start | bytes 1179656 | tf_op jit(solution)/shard_map/ppermute | solution.py:332
  4.8 0.0 collective-permute-done.near
  4.8 0.0 copy-done.1
  4.9 0.0 copy-done.2
  4.9 0.0 copy-done.3
  4.9 0.0 copy-done.4
  4.9 0.0 copy-done.5
  4.9 0.0 copy-start
  4.9 1.7 %copy-done = f32[4,5,8,16,256]{4,3,2,1,0:T(8,128)S(1)} copy-done((f32[4,5,8,16,256]{4,3,2,1,0:T(8,128)S(1)}, f32[4,5,8,16,256]{4,3,2,1,0:T(8,128)}, u32[]{:S(2)}) %copy-start) | copy-done | bytes 2621464
  6.6 3.7 %interior.1 = (f32[4,5,6,16,256]{4,3,2,1,0:T(8,128)S(1)}, f32[4,5,16,256]{3,2,1,0:T(8,128)S(1)}, f32[4,5,16,256]{3,2,1,0:T(8,128)S(1)}, f32[4,5,16,256]{3,2,1,0:...) custom-call(f32[4,5,8,16,256]{4,3,2,1,0:T(8,128)S(1)} %copy-done, ...), custom_call_target="tpu_custom_call" | custom-call | tf_op jit(solution)/shard_map/interior/pallas_call | solution.py:333
  10.4 3.0 %collective-permute-start.4 = (f32[4,2,2,16,256]{4,3,2,1,0:T(8,128)S(1)}, f32[4,2,2,16,256]{4,3,2,1,0:T(8,128)S(1)}, u32[]{:S(2)}, u32[]{:S(2)}) collective-permute-start(f32[4,2,2,16,256]{4,3,2,1,0:T(8,128)S(1)} %get-tuple-element.27), channel_id=1, source_target_pairs={{0,31},{1,2},{2,1},{3,4},{4,3},{5,6},{6,5},{7,8},{8,7},{9,10},{10,... | collective-permute-start | bytes 786440 | tf_op jit(solution)/shard_map/ppermute | solution.py:351
  13.4 0.0 collective-permute-done.1.far.far_winds_ref
  13.4 0.3 edges.1
  13.7 2.5 %collective-permute-start.3 = (f32[4,8,256]{2,1,0:T(8,128)S(1)}, f32[4,8,256]{2,1,0:T(8,128)S(1)}, u32[]{:S(2)}, u32[]{:S(2)}) collective-permute-start(f32[4,8,256]{2,1,0:T(8,128)S(1)} %get-tuple-element.24.own), channel_id=1, source_target_pairs={{0,31},{1,2},{2,1},{3,4},{4,3},{5,6},{6,5},{7,8},{8,7},{9,10},{10,... | collective-permute-start | bytes 98312 | tf_op jit(solution)/shard_map/ppermute | solution.py:365
  16.3 1.9 %collective-permute-start.2 = (f32[4,8,256]{2,1,0:T(8,128)S(1)}, f32[4,8,256]{2,1,0:T(8,128)S(1)}, u32[]{:S(2)}, u32[]{:S(2)}) collective-permute-start(f32[4,8,256]{2,1,0:T(8,128)S(1)} %get-tuple-element.24.own), channel_id=1, source_target_pairs={{0,1},{1,0},{2,3},{3,2},{4,5},{5,4},{6,7},{7,6},{8,9},{9,8},{10,11... | collective-permute-start | bytes 98312 | tf_op jit(solution)/shard_map/ppermute | solution.py:364
  18.2 1.8 %collective-permute-done.4.far = f32[4,2,2,16,256]{4,3,2,1,0:T(8,128)S(1)} collective-permute-done((f32[4,2,2,16,256]{4,3,2,1,0:T(8,128)S(1)}, f32[4,2,2,16,256]{4,3,2,1,0:T(8,128)S(1)}, u32[]{:S(2)}, u32[]{:S(2)}) %collective-permute-start.4) | collective-permute-done | bytes 262176 | tf_op jit(solution)/shard_map/ppermute | solution.py:351
  20.0 0.2 edges_rest.1.rest
  20.2 0.6 %collective-permute-done.3.beyond = f32[4,8,256]{2,1,0:T(8,128)S(1)} collective-permute-done((f32[4,8,256]{2,1,0:T(8,128)S(1)}, f32[4,8,256]{2,1,0:T(8,128)S(1)}, u32[]{:S(2)}, u32[]{:S(2)}) %collective-permute-start.3) | collective-permute-done | bytes 32800 | tf_op jit(solution)/shard_map/ppermute | solution.py:365
  20.8 0.0 collective-permute-done.2.beside
  20.8 1.0 %weights.1 = f32[8,88,256]{2,1,0:T(8,128)S(1)} custom-call(s32[16,256]{1,0:T(8,128)S(1)} %get-tuple-element.17.level_radius, f32[4,8,256]{2,1,0:T(8,128)S(1)} %get-tuple-element.24.own, f32[4,8,256]{2,1,0:T(8,128)S(1)} %collective-permute-done.2.beside, f32[4,8,256]{2,1,0:T(8,128)S(1)} %collective-permute-done.3.beyond, ...), custom_call_target="tpu_custom_call" | custom-call | tf_op jit(solution)/shard_map/weights/pallas_call | solution.py:373
  21.8 16.9 %all_to_all.10.parts = f32[8,88,256]{2,1,0:T(8,128)S(1)} all-to-all(f32[8,88,256]{2,1,0:T(8,128)S(1)} %weights.1), channel_id=1, replica_groups={{0,64,128,192,32,96,160,224},{193,129,65,1,225,161,97,33},{2,66,130,194..., dimensions={0} | all-to-all | bytes 1441792 | tf_op jit(solution)/shard_map/all_to_all | solution.py:385
  38.8 0.1 combine.1
  38.9 13.8 %all_to_all.11.mean = f32[8,80,256]{2,1,0:T(8,128)S(1)} all-to-all(f32[8,80,256]{2,1,0:T(8,128)S(1)} %combine.1), channel_id=1, replica_groups={{0,64,128,192,32,96,160,224},{193,129,65,1,225,161,97,33},{2,66,130,194..., dimensions={0} | all-to-all | bytes 1310720 | tf_op jit(solution)/shard_map/all_to_all | solution.py:393
  52.7 1.6 %blend.1 = f32[4,5,8,16,256]{4,3,2,1,0:T(8,128)} custom-call(f32[8,80,256]{2,1,0:T(8,128)S(1)} %all_to_all.11.mean, f32[4,5,6,16,256]{4,3,2,1,0:T(8,128)S(1)} %get-tuple-element.25.core, f32[4,3,2,16,256]{4,3,2,1,0:T(8,128)S(1)} %get-tuple-element.26.edge, f32[4,2,2,16,256]{4,3,2,1,0:T(8,128)S(1)} %edges_rest.1.rest), custom_call_target="tpu_custom_call" | custom-call | tf_op jit(solution)/shard_map/blend/pallas_call | solution.py:394
  (2 shorter events, 0.0 us)
Async XLA Ops:
  0.0 1.6 %slice-start = ((f32[4,5,8,16,256]{4,3,2,1,0:T(8,128)}), f32[4,3,8,16,256]{4,3,2,1,0:T(8,128)S(1)}, s32[]{:S(2)}) async-start(f32[4,5,8,16,256]{4,3,2,1,0:T(8,128)} %state.5), calls=%async_computation.2 | async-start | bytes 3145728 | tf_op jit(solution)/shard_map/slice | solution.py:330
  0.0 4.8 %copy-start.1 = (f32[5]{0:T(128)S(1)}, f32[5]{0:T(128)}, u32[]{:S(2)}) copy-start(f32[5]{0:T(128)} %diffusion.1) | copy-start | bytes 64
  0.0 4.9 %copy-start.2 = (s32[16]{0:T(128)S(1)}, s32[16]{0:T(128)}, u32[]{:S(2)}) copy-start(s32[16]{0:T(128)} %radius.1) | copy-start | bytes 196
  0.0 4.9 %copy-start.3 = (s32[1,128]{1,0:T(1,128)S(1)}, s32[1,128]{1,0:T(1,128)}, u32[]{:S(2)}) copy-start(s32[1,128]{1,0:T(1,128)} %cells.1) | copy-start | bytes 1540
  0.0 4.9 %copy-start.4 = (f32[1,128]{1,0:T(1,128)S(1)}, f32[1,128]{1,0:T(1,128)}, u32[]{:S(2)}) copy-start(f32[1,128]{1,0:T(1,128)} %value.1) | copy-start | bytes 1540
  0.0 4.9 %copy-start.5 = (f32[1,128]{1,0:T(1,128)S(1)}, f32[1,128]{1,0:T(1,128)}, u32[]{:S(2)}) copy-start(f32[1,128]{1,0:T(1,128)} %error.1) | copy-start | bytes 1540
  1.3 3.5 %collective-permute-start = (f32[4,5,2,16,256]{4,3,2,1,0:T(8,128)S(1)}, f32[4,5,2,16,256]{4,3,2,1,0:T(8,128)S(1)}, u32[]{:S(2)}, u32[]{:S(2)}) collective-permute-start(f32[4,5,2,16,256]{4,3,2,1,0:T(8,128)S(1)} %constant_dynamic-slice_fusion.1), channel_id=1, source_target_pairs={{0,1},{1,0},{2,3},{3,2},{4,5},{5,4},{6,7},{7,6},{8,9},{9,8},{10,11... | collective-permute-start | bytes 1966088 | tf_op jit(solution)/shard_map/ppermute | solution.py:331
  1.6 11.7 %collective-permute-start.1 = (f32[4,3,2,16,256]{4,3,2,1,0:T(8,128)S(1)}, f32[4,3,2,16,256]{4,3,2,1,0:T(8,128)S(1)}, u32[]{:S(2)}, u32[]{:S(2)}) collective-permute-start(f32[4,3,2,16,256]{4,3,2,1,0:T(8,128)S(1)} %constant_dynamic-slice_fusion), channel_id=1, source_target_pairs={{0,31},{1,2},{2,1},{3,4},{4,3},{5,6},{6,5},{7,8},{8,7},{9,10},{10,... | collective-permute-start | bytes 1179656 | tf_op jit(solution)/shard_map/ppermute | solution.py:332
  4.9 1.7 %copy-start = (f32[4,5,8,16,256]{4,3,2,1,0:T(8,128)S(1)}, f32[4,5,8,16,256]{4,3,2,1,0:T(8,128)}, u32[]{:S(2)}) copy-start(f32[4,5,8,16,256]{4,3,2,1,0:T(8,128)} %state.5) | copy-start | bytes 7864324
  10.4 9.6 %collective-permute-start.4 = (f32[4,2,2,16,256]{4,3,2,1,0:T(8,128)S(1)}, f32[4,2,2,16,256]{4,3,2,1,0:T(8,128)S(1)}, u32[]{:S(2)}, u32[]{:S(2)}) collective-permute-start(f32[4,2,2,16,256]{4,3,2,1,0:T(8,128)S(1)} %get-tuple-element.27), channel_id=1, source_target_pairs={{0,31},{1,2},{2,1},{3,4},{4,3},{5,6},{6,5},{7,8},{8,7},{9,10},{10,... | collective-permute-start | bytes 786440 | tf_op jit(solution)/shard_map/ppermute | solution.py:351
  13.7 7.0 %collective-permute-start.3 = (f32[4,8,256]{2,1,0:T(8,128)S(1)}, f32[4,8,256]{2,1,0:T(8,128)S(1)}, u32[]{:S(2)}, u32[]{:S(2)}) collective-permute-start(f32[4,8,256]{2,1,0:T(8,128)S(1)} %get-tuple-element.24.own), channel_id=1, source_target_pairs={{0,31},{1,2},{2,1},{3,4},{4,3},{5,6},{6,5},{7,8},{8,7},{9,10},{10,... | collective-permute-start | bytes 98312 | tf_op jit(solution)/shard_map/ppermute | solution.py:365
  16.3 4.5 %collective-permute-start.2 = (f32[4,8,256]{2,1,0:T(8,128)S(1)}, f32[4,8,256]{2,1,0:T(8,128)S(1)}, u32[]{:S(2)}, u32[]{:S(2)}) collective-permute-start(f32[4,8,256]{2,1,0:T(8,128)S(1)} %get-tuple-element.24.own), channel_id=1, source_target_pairs={{0,1},{1,0},{2,3},{3,2},{4,5},{5,4},{6,7},{7,6},{8,9},{9,8},{10,11... | collective-permute-start | bytes 98312 | tf_op jit(solution)/shard_map/ppermute | solution.py:364
